TPU v7x, 256 devices: a whole 4x4x8 slice. The times are simulated.
256 devices in a mesh: seq: 32 (over z, y_hi, core), head: 8 (over x, y_lo).
Axes of the slice: x: 4, y: 4 (y_hi: 2, y_lo: 2; y = y_hi * 2 + y_lo), z: 8, core: 2. Of those that a mesh axis runs over, the one named last changes fastest.
Arguments:
- query_raw: bfloat16 [8192, 8192], P('seq', 'head'), may hold values from -208 to 208
- key_raw: bfloat16 [8192, 8192], P('seq', 'head'), may hold values from -208 to 208
- values: bfloat16 [8192, 8192], P('seq', 'head'), may hold values from -6 to 6
- out_grad: bfloat16 [8192, 8192], P('seq', 'head'), may hold values from -6 to 6
- attn_out: bfloat16 [8192, 8192], P('seq', 'head'), may hold values from -4 to 4
- log_norm: float32 [64, 8192], P('head', 'seq'), may hold values from 6 to 10
- query_gain: float32 [8192], P('head'), may hold values from 0.1 to 1.9
- key_gain: float32 [8192], P('head'), may hold values from 0.1 to 1.9
- block_order: int32 [64], replicated, may hold values from 0 to 63, as said below
Outputs:
- query_grad: bfloat16 [8192, 8192], P('seq', 'head')
- key_grad: bfloat16 [8192, 8192], P('seq', 'head')
- value_grad: bfloat16 [8192, 8192], P('seq', 'head')
Inputs may be any that keep to these rules, and one draw needn't show every extreme that they name: block_order is a permutation of 0 to 63; stored blocks 2 g and 2 g + 1 of each group g hold positions p and 63 - p, in either order, for some p below 32.
All inputs are finite; a program needn't handle non-finite values.
Results may differ from a plain program's by a relative error of at most 0.012.
Values may be sent and summed in bfloat16 or wider, within the bound.
A program may use at most 64 MiB of HBM per device.

v0:
```python
import jax
import jax.numpy as jnp
from jax import lax
from jax.sharding import PartitionSpec as P

WINDOW = 4


EPSILON = 1e-06


def passed_along(value, axis, by):
    peers = lax.axis_size(axis)
    return lax.ppermute(value, axis, [(i, (i + by) % peers) for i in range(peers)])


def rows_of(order_all, group, block_len):
    starts = lax.dynamic_slice_in_dim(order_all, group * 2, 2)
    return starts[:, None] * block_len + jnp.arange(block_len, dtype=jnp.int32)[None, :]


def pair_terms(
    query_block,
    grad_block,
    delta_block,
    norm_block,
    query_pos,
    key_block,
    value_block,
    key_pos,
    score_scale,
):
    scores = (
        jnp.einsum("qhd,khd->hqk", query_block, key_block, preferred_element_type=jnp.float32)
        * score_scale
    )
    visible = key_pos[None, None, :] <= query_pos[None, :, None]
    probs = jnp.where(visible, jnp.exp(scores - norm_block[:, :, None]), 0.0)
    dprobs = jnp.einsum("qhd,khd->hqk", grad_block, value_block, preferred_element_type=jnp.float32)
    dscores = probs * (dprobs - delta_block[:, :, None])
    probs_low = probs.astype(jnp.bfloat16)
    dscores_low = dscores.astype(jnp.bfloat16)
    query_add = (
        jnp.einsum("hqk,khd->qhd", dscores_low, key_block, preferred_element_type=jnp.float32)
        * score_scale
    )
    key_add = (
        jnp.einsum("hqk,qhd->khd", dscores_low, query_block, preferred_element_type=jnp.float32)
        * score_scale
    )
    value_add = jnp.einsum(
        "hqk,qhd->khd", probs_low, grad_block, preferred_element_type=jnp.float32
    )
    return (query_add, key_add, value_add)


def window(
    query_in, grad_in, delta_in, norm_in, query_pos, keys_in, values_in, key_pos, score_scale
):
    empty = jnp.zeros(query_in.shape[1:], jnp.float32)
    query_parts = [empty, empty]
    key_parts = []
    value_parts = []
    for key_idx in range(2):
        key_sum = empty
        value_sum = empty
        for query_idx in range(2):
            terms = pair_terms(
                query_in[query_idx],
                grad_in[query_idx],
                delta_in[query_idx],
                norm_in[query_idx],
                query_pos[query_idx],
                keys_in[key_idx],
                values_in[key_idx],
                key_pos[key_idx],
                score_scale,
            )
            query_parts[query_idx] = query_parts[query_idx] + terms[0]
            key_sum = key_sum + terms[1]
            value_sum = value_sum + terms[2]
        key_parts.append(key_sum)
        value_parts.append(value_sum)
    return (jnp.stack(query_parts), jnp.stack(key_parts), jnp.stack(value_parts))


def local(
    query_raw, key_raw, values, out_grad, attn_out, log_norm, query_gain, key_gain, block_order
):
    tok_rows, columns = query_raw.shape
    head_count = log_norm.shape[0]
    head_dim = columns // head_count
    block_len = tok_rows // 2
    score_scale = head_dim ** (-0.5)
    full_width = columns * lax.axis_size("head")
    seq_count = lax.axis_size("seq")
    device = lax.axis_index("seq")
    query_wide = query_raw.astype(jnp.float32)
    key_wide = key_raw.astype(jnp.float32)
    squares = lax.psum(
        (jnp.sum(query_wide * query_wide, axis=1), jnp.sum(key_wide * key_wide, axis=1)), "head"
    )
    query_scale = lax.rsqrt(squares[0] / full_width + EPSILON)
    key_scale = lax.rsqrt(squares[1] / full_width + EPSILON)
    query_normed = (query_wide * query_scale[:, None] * query_gain[None, :]).astype(jnp.bfloat16)
    key_normed = (key_wide * key_scale[:, None] * key_gain[None, :]).astype(jnp.bfloat16)
    shape_four = (2, block_len, head_count, head_dim)
    query_pair = query_normed.reshape(shape_four)
    key_pair = key_normed.reshape(shape_four)
    value_pair = values.reshape(shape_four)
    grad_pair = out_grad.reshape(shape_four)
    products = out_grad.astype(jnp.float32) * attn_out.astype(jnp.float32)
    row_delta = jnp.sum(products.reshape(tok_rows, head_count, head_dim), axis=2)
    row_delta = row_delta.reshape(2, block_len, head_count).transpose(0, 2, 1)
    norm_pair = log_norm.reshape(head_count, 2, block_len).transpose(1, 0, 2)
    own_pos = rows_of(block_order, device, block_len)
    zero_four = jnp.zeros(shape_four, jnp.float32)
    moving = (key_pair, value_pair)
    query_total = zero_four
    carried = (zero_four, zero_four)
    key_total = zero_four
    value_total = zero_four
    for cycle_step in range(WINDOW):
        if cycle_step > 0:
            moving = passed_along((moving[0], moving[1]), "seq", 1)
        key_group = (device - cycle_step) % seq_count
        key_pos = rows_of(block_order, key_group, block_len)
        query_add, key_add, value_add = window(
            query_pair,
            grad_pair,
            row_delta,
            norm_pair,
            own_pos,
            moving[0],
            moving[1],
            key_pos,
            score_scale,
        )
        query_total = query_total + query_add
        if cycle_step == 0:
            carried = (key_add, value_add)
        else:
            carried = (carried[0] + key_add, carried[1] + value_add)
        if cycle_step + 1 < WINDOW:
            carried = passed_along((carried[0], carried[1]), "seq", 1)
        else:
            key_total, value_total = (
                passed_along(carried[0].astype(jnp.bfloat16), "seq", 1 - WINDOW).astype(
                    jnp.float32
                ),
                passed_along(carried[1].astype(jnp.bfloat16), "seq", 1 - WINDOW).astype(
                    jnp.float32
                ),
            )
    query_grad = query_total.reshape(tok_rows, columns).astype(jnp.bfloat16)
    key_grad = key_total.reshape(tok_rows, columns).astype(jnp.bfloat16)
    value_grad = value_total.reshape(tok_rows, columns).astype(jnp.bfloat16)
    return (query_grad, key_grad, value_grad)


def solution(mesh):
    placed = (
        P("seq", "head"),
        P("seq", "head"),
        P("seq", "head"),
        P("seq", "head"),
        P("seq", "head"),
        P("head", "seq"),
        P("head"),
        P("head"),
        P(),
    )
    return jax.shard_map(
        local,
        mesh=mesh,
        in_specs=placed,
        out_specs=(P("seq", "head"), P("seq", "head"), P("seq", "head")),
        check_vma=False,
    )
```

profile of v0, /device:TPU:1, one launch (start us, length us, event | category | flops | bytes accessed | tf_op | source)
XLA Modules:
  0.0 180.8 jit_solution(6315918837145090040)
XLA Ops:
  1.7 1.2 copy.156
  4.4 16.8 %all-reduce = (f32[256]{0:T(256)S(1)}, f32[256]{0:T(256)S(1)}) all-reduce(f32[256]{0:T(256)S(1)} %fusion.120, f32[256]{0:T(256)S(1)} %fusion.123), channel_id=1, replica_groups=mesh['seq'=32,'head'=8] {'head'}, use_global_device_ids=true, to_apply=%region_1.0 | all-reduce | flops 512 | bytes 4096 | tf_op jit(solution)/shard_map/psum | solution.py:100
  29.9 6.9 %collective-permute-start.10 = (f32[2,128,8,128]{3,1,2,0:T(8,128)}, f32[2,128,8,128]{3,1,2,0:T(8,128)}, u32[]{:S(2)}, u32[]{:S(2)}) collective-permute-start(f32[2,128,8,128]{3,1,2,0:T(8,128)} %pad_maximum_fusion.1), channel_id=1, source_target_pairs={{0,8},{8,16},{16,24},{24,32},{32,40},{40,48},{48,56},{56,64},{64,7... | collective-permute-start | bytes 3145736 | tf_op jit(solution)/shard_map/ppermute | solution.py:14
  37.7 2.1 %copy.180 = bf16[2,128,8,128]{3,1,2,0:T(8,128)(2,1)} copy(bf16[2,128,8,128]{1,0,3,2:T(2,128)(2,1)} %reshape.585) | data formatting | bytes 1048576 | tf_op jit(solution)/shard_map/reshape | solution.py:109
  39.8 1.2 multiply_bitcast_fusion
  41.0 1.2 copy.343
  42.2 1.6 reduce_sum.29
  44.7 1.2 copy.341
  48.0 1.2 copy.340
  52.2 2.2 %collective-permute-start.6 = (f32[2,128,8,128]{1,3,2,0:T(8,128)S(1)}, f32[2,128,8,128]{1,3,2,0:T(8,128)S(1)}, u32[]{:S(2)}, u32[]{:S(2)}) collective-permute-start(f32[2,128,8,128]{1,3,2,0:T(8,128)S(1)} %pad_maximum_fusion), channel_id=1, source_target_pairs={{0,8},{8,16},{16,24},{24,32},{32,40},{40,48},{48,56},{56,64},{64,7... | collective-permute-start | bytes 3145736 | tf_op jit(solution)/shard_map/ppermute | solution.py:14
  54.6 1.1 collective-permute-start.1
  57.3 1.3 fusion.77
  58.9 12.8 %collective-permute-done.1 = bf16[2,128,8,128]{3,1,2,0:T(8,128)(2,1)S(1)} collective-permute-done((bf16[2,128,8,128]{3,1,2,0:T(8,128)(2,1)S(1)}, bf16[2,128,8,128]{3,1,2,0:T(8,128)(2,1)S(1)}, u32[]{:S(2)}, u32[]{:S(2)}) %collective-permute-start.1) | collective-permute-done | bytes 524320 | tf_op jit(solution)/shard_map/ppermute | solution.py:14
  72.8 1.3 fusion.83
  75.1 1.3 fusion.67
  77.0 4.1 %collective-permute-start.2 = (bf16[2,128,8,128]{3,1,2,0:T(8,128)(2,1)}, bf16[2,128,8,128]{3,1,2,0:T(8,128)(2,1)S(1)}, u32[]{:S(2)}, u32[]{:S(2)}) collective-permute-start(bf16[2,128,8,128]{3,1,2,0:T(8,128)(2,1)} %collective-permute-done), channel_id=1, source_target_pairs={{0,8},{8,16},{16,24},{24,32},{32,40},{40,48},{48,56},{56,64},{64,7... | collective-permute-start | bytes 1572872 | tf_op jit(solution)/shard_map/ppermute | solution.py:14
  81.1 1.3 fusion.156
  82.4 1.3 fusion.155
  83.7 1.3 fusion.73
  85.5 1.3 fusion.79
  86.8 1.3 fusion.69
  89.1 1.3 maximum_add_fusion.4
  90.5 3.9 %collective-permute-start.11 = (f32[2,128,8,128]{3,1,2,0:T(8,128)S(1)}, f32[2,128,8,128]{3,1,2,0:T(8,128)S(1)}, u32[]{:S(2)}, u32[]{:S(2)}) collective-permute-start(f32[2,128,8,128]{3,1,2,0:T(8,128)S(1)} %maximum_add_fusion.4), channel_id=1, source_target_pairs={{0,8},{8,16},{16,24},{24,32},{32,40},{40,48},{48,56},{56,64},{64,7... | collective-permute-start | bytes 3145736 | tf_op jit(solution)/shard_map/ppermute | solution.py:14
  98.9 1.4 collective-permute-start.4
  102.5 20.5 %collective-permute-done.4 = bf16[2,128,8,128]{3,1,2,0:T(8,128)(2,1)S(1)} collective-permute-done((bf16[2,128,8,128]{3,1,2,0:T(8,128)(2,1)S(1)}, bf16[2,128,8,128]{3,1,2,0:T(8,128)(2,1)S(1)}, u32[]{:S(2)}, u32[]{:S(2)}) %collective-permute-start.4) | collective-permute-done | bytes 524320 | tf_op jit(solution)/shard_map/ppermute | solution.py:14
  123.3 5.3 %collective-permute-done.5 = bf16[2,128,8,128]{3,1,2,0:T(8,128)(2,1)S(1)} collective-permute-done((bf16[2,128,8,128]{3,1,2,0:T(8,128)(2,1)S(1)}, bf16[2,128,8,128]{3,1,2,0:T(8,128)(2,1)S(1)}, u32[]{:S(2)}, u32[]{:S(2)}) %collective-permute-start.5) | collective-permute-done | bytes 524320 | tf_op jit(solution)/shard_map/ppermute | solution.py:14
  132.4 4.1 %collective-permute-start.12 = (f32[2,128,8,128]{3,1,2,0:T(8,128)S(1)}, f32[2,128,8,128]{3,1,2,0:T(8,128)S(1)}, u32[]{:S(2)}, u32[]{:S(2)}) collective-permute-start(f32[2,128,8,128]{3,1,2,0:T(8,128)S(1)} %maximum_add_fusion.5), channel_id=1, source_target_pairs={{0,8},{8,16},{16,24},{24,32},{32,40},{40,48},{48,56},{56,64},{64,7... | collective-permute-start | bytes 3145736 | tf_op jit(solution)/shard_map/ppermute | solution.py:14
  138.3 9.9 %collective-permute-done.12 = f32[2,128,8,128]{3,1,2,0:T(8,128)S(1)} collective-permute-done((f32[2,128,8,128]{3,1,2,0:T(8,128)S(1)}, f32[2,128,8,128]{3,1,2,0:T(8,128)S(1)}, u32[]{:S(2)}, u32[]{:S(2)}) %collective-permute-start.12) | collective-permute-done | bytes 1048608 | tf_op jit(solution)/shard_map/ppermute | solution.py:14
  148.4 7.0 %collective-permute-start.13 = (bf16[2,128,8,128]{3,1,2,0:T(8,128)(2,1)S(1)}, bf16[2,128,8,128]{3,1,2,0:T(8,128)(2,1)S(1)}, u32[]{:S(2)}, u32[]{:S(2)}) collective-permute-start(bf16[2,128,8,128]{3,1,2,0:T(8,128)(2,1)S(1)} %fusion.130), channel_id=1, source_target_pairs={{0,232},{8,240},{16,248},{24,0},{32,8},{40,16},{48,24},{56,32},{64... | collective-permute-start | bytes 1572872 | tf_op jit(solution)/shard_map/ppermute | solution.py:14
  155.4 9.6 %collective-permute-done.8 = f32[2,128,8,128]{1,3,2,0:T(8,128)S(1)} collective-permute-done((f32[2,128,8,128]{1,3,2,0:T(8,128)S(1)}, f32[2,128,8,128]{1,3,2,0:T(8,128)S(1)}, u32[]{:S(2)}, u32[]{:S(2)}) %collective-permute-start.8) | collective-permute-done | bytes 1048608 | tf_op jit(solution)/shard_map/ppermute | solution.py:14
  165.1 6.0 %collective-permute-start.9 = (bf16[2,128,8,128]{1,3,2,0:T(8,128)(2,1)S(1)}, bf16[2,128,8,128]{1,3,2,0:T(8,128)(2,1)S(1)}, u32[]{:S(2)}, u32[]{:S(2)}) collective-permute-start(bf16[2,128,8,128]{1,3,2,0:T(8,128)(2,1)S(1)} %fusion.129), channel_id=1, source_target_pairs={{0,232},{8,240},{16,248},{24,0},{32,8},{40,16},{48,24},{56,32},{64... | collective-permute-start | bytes 1572872 | tf_op jit(solution)/shard_map/ppermute | solution.py:14
  174.5 5.0 %collective-permute-done.9 = bf16[2,128,8,128]{1,3,2,0:T(8,128)(2,1)S(1)} collective-permute-done((bf16[2,128,8,128]{1,3,2,0:T(8,128)(2,1)S(1)}, bf16[2,128,8,128]{1,3,2,0:T(8,128)(2,1)S(1)}, u32[]{:S(2)}, u32[]{:S(2)}) %collective-permute-start.9) | collective-permute-done | bytes 524320 | tf_op jit(solution)/shard_map/ppermute | solution.py:14
  (165 shorter events, 41.6 us)
Async XLA Ops:
  2.9 1.0 copy-start.10
  21.1 0.7 copy-start.17
  22.0 0.7 copy-start.18
  22.9 0.7 copy-start.16
  23.0 1.0 copy-start.8
  25.6 0.8 copy-start.2
  26.7 0.8 copy-start
  29.9 59.2 %collective-permute-start.10 = (f32[2,128,8,128]{3,1,2,0:T(8,128)}, f32[2,128,8,128]{3,1,2,0:T(8,128)}, u32[]{:S(2)}, u32[]{:S(2)}) collective-permute-start(f32[2,128,8,128]{3,1,2,0:T(8,128)} %pad_maximum_fusion.1), channel_id=1, source_target_pairs={{0,8},{8,16},{16,24},{24,32},{32,40},{40,48},{48,56},{56,64},{64,7... | collective-permute-start | bytes 3145736 | tf_op jit(solution)/shard_map/ppermute | solution.py:14
  37.7 2.1 %copy-start.9 = (bf16[256,1024]{1,0:T(8,128)(2,1)S(1)}, bf16[256,1024]{1,0:T(8,128)(2,1)}, u32[]{:S(2)}) copy-start(bf16[256,1024]{1,0:T(8,128)(2,1)} %param.12) | copy-start | bytes 1572868
  39.8 17.1 %collective-permute-start = (bf16[2,128,8,128]{3,1,2,0:T(8,128)(2,1)}, bf16[2,128,8,128]{3,1,2,0:T(8,128)(2,1)}, u32[]{:S(2)}, u32[]{:S(2)}) collective-permute-start(bf16[2,128,8,128]{3,1,2,0:T(8,128)(2,1)} %copy.180), channel_id=1, source_target_pairs={{0,8},{8,16},{16,24},{24,32},{32,40},{40,48},{48,56},{56,64},{64,7... | collective-permute-start | bytes 1572872 | tf_op jit(solution)/shard_map/ppermute | solution.py:14
  42.2 1.7 copy-start.6
  44.7 1.2 copy-start.3
  48.0 1.2 copy-start.1
  49.5 1.0 copy-start.5
  50.7 1.0 copy-start.4
  52.1 2.3 %copy-start.7 = (bf16[256,1024]{1,0:T(8,128)(2,1)S(1)}, bf16[256,1024]{1,0:T(8,128)(2,1)}, u32[]{:S(2)}) copy-start(bf16[256,1024]{1,0:T(8,128)(2,1)} %param.11) | copy-start | bytes 1572868
  52.2 42.2 %collective-permute-start.6 = (f32[2,128,8,128]{1,3,2,0:T(8,128)S(1)}, f32[2,128,8,128]{1,3,2,0:T(8,128)S(1)}, u32[]{:S(2)}, u32[]{:S(2)}) collective-permute-start(f32[2,128,8,128]{1,3,2,0:T(8,128)S(1)} %pad_maximum_fusion), channel_id=1, source_target_pairs={{0,8},{8,16},{16,24},{24,32},{32,40},{40,48},{48,56},{56,64},{64,7... | collective-permute-start | bytes 3145736 | tf_op jit(solution)/shard_map/ppermute | solution.py:14
  54.6 17.2 %collective-permute-start.1 = (bf16[2,128,8,128]{3,1,2,0:T(8,128)(2,1)S(1)}, bf16[2,128,8,128]{3,1,2,0:T(8,128)(2,1)S(1)}, u32[]{:S(2)}, u32[]{:S(2)}) collective-permute-start(bf16[2,128,8,128]{3,1,2,0:T(8,128)(2,1)S(1)} %copy.182), channel_id=1, source_target_pairs={{0,8},{8,16},{16,24},{24,32},{32,40},{40,48},{48,56},{56,64},{64,7... | collective-permute-start | bytes 1572872 | tf_op jit(solution)/shard_map/ppermute | solution.py:14
  56.6 0.7 copy-start.14
  72.1 0.7 copy-start.13
  74.4 0.7 copy-start.12
  77.0 17.7 %collective-permute-start.2 = (bf16[2,128,8,128]{3,1,2,0:T(8,128)(2,1)}, bf16[2,128,8,128]{3,1,2,0:T(8,128)(2,1)S(1)}, u32[]{:S(2)}, u32[]{:S(2)}) collective-permute-start(bf16[2,128,8,128]{3,1,2,0:T(8,128)(2,1)} %collective-permute-done), channel_id=1, source_target_pairs={{0,8},{8,16},{16,24},{24,32},{32,40},{40,48},{48,56},{56,64},{64,7... | collective-permute-start | bytes 1572872 | tf_op jit(solution)/shard_map/ppermute | solution.py:14
  81.0 15.0 %collective-permute-start.3 = (bf16[2,128,8,128]{3,1,2,0:T(8,128)(2,1)S(1)}, bf16[2,128,8,128]{3,1,2,0:T(8,128)(2,1)S(1)}, u32[]{:S(2)}, u32[]{:S(2)}) collective-permute-start(bf16[2,128,8,128]{3,1,2,0:T(8,128)(2,1)S(1)} %collective-permute-done.1), channel_id=1, source_target_pairs={{0,8},{8,16},{16,24},{24,32},{32,40},{40,48},{48,56},{56,64},{64,7... | collective-permute-start | bytes 1572872 | tf_op jit(solution)/shard_map/ppermute | solution.py:14
  82.4 1.3 copy-start.11
  90.5 41.8 %collective-permute-start.11 = (f32[2,128,8,128]{3,1,2,0:T(8,128)S(1)}, f32[2,128,8,128]{3,1,2,0:T(8,128)S(1)}, u32[]{:S(2)}, u32[]{:S(2)}) collective-permute-start(f32[2,128,8,128]{3,1,2,0:T(8,128)S(1)} %maximum_add_fusion.4), channel_id=1, source_target_pairs={{0,8},{8,16},{16,24},{24,32},{32,40},{40,48},{48,56},{56,64},{64,7... | collective-permute-start | bytes 3145736 | tf_op jit(solution)/shard_map/ppermute | solution.py:14
  94.5 42.0 %collective-permute-start.7 = (f32[2,128,8,128]{1,3,2,0:T(8,128)S(1)}, f32[2,128,8,128]{1,3,2,0:T(8,128)S(1)}, u32[]{:S(2)}, u32[]{:S(2)}) collective-permute-start(f32[2,128,8,128]{1,3,2,0:T(8,128)S(1)} %maximum_add_fusion.1), channel_id=1, source_target_pairs={{0,8},{8,16},{16,24},{24,32},{32,40},{40,48},{48,56},{56,64},{64,7... | collective-permute-start | bytes 3145736 | tf_op jit(solution)/shard_map/ppermute | solution.py:14
  98.9 24.0 %collective-permute-start.4 = (bf16[2,128,8,128]{3,1,2,0:T(8,128)(2,1)S(1)}, bf16[2,128,8,128]{3,1,2,0:T(8,128)(2,1)S(1)}, u32[]{:S(2)}, u32[]{:S(2)}) collective-permute-start(bf16[2,128,8,128]{3,1,2,0:T(8,128)(2,1)S(1)} %collective-permute-done.2), channel_id=1, source_target_pairs={{0,8},{8,16},{16,24},{24,32},{32,40},{40,48},{48,56},{56,64},{64,7... | collective-permute-start | bytes 1572872 | tf_op jit(solution)/shard_map/ppermute | solution.py:14
  100.3 28.2 %collective-permute-start.5 = (bf16[2,128,8,128]{3,1,2,0:T(8,128)(2,1)S(1)}, bf16[2,128,8,128]{3,1,2,0:T(8,128)(2,1)S(1)}, u32[]{:S(2)}, u32[]{:S(2)}) collective-permute-start(bf16[2,128,8,128]{3,1,2,0:T(8,128)(2,1)S(1)} %collective-permute-done.3), channel_id=1, source_target_pairs={{0,8},{8,16},{16,24},{24,32},{32,40},{40,48},{48,56},{56,64},{64,7... | collective-permute-start | bytes 1572872 | tf_op jit(solution)/shard_map/ppermute | solution.py:14
  132.4 15.8 %collective-permute-start.12 = (f32[2,128,8,128]{3,1,2,0:T(8,128)S(1)}, f32[2,128,8,128]{3,1,2,0:T(8,128)S(1)}, u32[]{:S(2)}, u32[]{:S(2)}) collective-permute-start(f32[2,128,8,128]{3,1,2,0:T(8,128)S(1)} %maximum_add_fusion.5), channel_id=1, source_target_pairs={{0,8},{8,16},{16,24},{24,32},{32,40},{40,48},{48,56},{56,64},{64,7... | collective-permute-start | bytes 3145736 | tf_op jit(solution)/shard_map/ppermute | solution.py:14
  136.6 28.3 %collective-permute-start.8 = (f32[2,128,8,128]{1,3,2,0:T(8,128)S(1)}, f32[2,128,8,128]{1,3,2,0:T(8,128)S(1)}, u32[]{:S(2)}, u32[]{:S(2)}) collective-permute-start(f32[2,128,8,128]{1,3,2,0:T(8,128)S(1)} %maximum_add_fusion.2), channel_id=1, source_target_pairs={{0,8},{8,16},{16,24},{24,32},{32,40},{40,48},{48,56},{56,64},{64,7... | collective-permute-start | bytes 3145736 | tf_op jit(solution)/shard_map/ppermute | solution.py:14
  148.4 24.9 %collective-permute-start.13 = (bf16[2,128,8,128]{3,1,2,0:T(8,128)(2,1)S(1)}, bf16[2,128,8,128]{3,1,2,0:T(8,128)(2,1)S(1)}, u32[]{:S(2)}, u32[]{:S(2)}) collective-permute-start(bf16[2,128,8,128]{3,1,2,0:T(8,128)(2,1)S(1)} %fusion.130), channel_id=1, source_target_pairs={{0,232},{8,240},{16,248},{24,0},{32,8},{40,16},{48,24},{56,32},{64... | collective-permute-start | bytes 1572872 | tf_op jit(solution)/shard_map/ppermute | solution.py:14
  165.1 14.5 %collective-permute-start.9 = (bf16[2,128,8,128]{1,3,2,0:T(8,128)(2,1)S(1)}, bf16[2,128,8,128]{1,3,2,0:T(8,128)(2,1)S(1)}, u32[]{:S(2)}, u32[]{:S(2)}) collective-permute-start(bf16[2,128,8,128]{1,3,2,0:T(8,128)(2,1)S(1)} %fusion.129), channel_id=1, source_target_pairs={{0,232},{8,240},{16,248},{24,0},{32,8},{40,16},{48,24},{56,32},{64... | collective-permute-start | bytes 1572872 | tf_op jit(solution)/shard_map/ppermute | solution.py:14
  (1 other events, 0.7 us)
where the time goes:
time: 184 us; the launch traced here: 181 us
  waiting for transfers between devices  63.1 us (34%)
  starting transfers between devices  37.2 us (20%)
  matrix products  33.5 us (18%)
  local copies, waits for them, and re-layouts  20.6 us (11%)
  blocking collectives  16.8 us (9%)
  other arithmetic  8.16 us (4%)
    ppermute x14, waiting for transfers between devices, passed_along(): lax.ppermute(value, axis, [(i, (i + by) % peers) for i in range(peers)])  63.1 us
    ppermute x14, starting transfers between devices, passed_along(): lax.ppermute(value, axis, [(i, (i + by) % peers) for i in range(peers)])  37.2 us
    psum x1, blocking collectives, local(): lax.psum((jnp.sum(query_wide * query_wide, axis=1), jnp.sum(key_wide * ke...  16.8 us
    unnamed x49, local copies, waits for them, and re-layouts  15.6 us
    dot_general x16, matrix products, pair_terms(): jnp.einsum('qhd,khd->hqk', query_block, key_block, preferred_element_type...  9.15 us
    dot_general x16, matrix products, pair_terms(): jnp.einsum('hqk,khd->qhd', dscores_low, key_block, preferred_element_type...  8.99 us
    dot_general x16, matrix products, pair_terms(): jnp.einsum('qhd,khd->hqk', grad_block, value_block, preferred_element_typ...  6.64 us
    dot_general x16, matrix products, pair_terms(): jnp.einsum('hqk,qhd->khd', probs_low, grad_block, preferred_element_type=...  5.32 us
  transfers between devices with their start and end apart: 14, of which 6 were waited for; matrix products, arithmetic and copies ran while one was open for 26% of the time, Pallas kernels for 0%

commit v1 on v0

v1 whole, which is shorter than its diff:
```python
import functools

import jax
import jax.numpy as jnp
from jax import lax
from jax.experimental import pallas as pl
from jax.experimental.pallas import tpu as pltpu
from jax.sharding import PartitionSpec as P

EPSILON = 1e-06
LOG2E = 1.4426950408889634
MESH = pl.DeviceIdType.MESH
F32 = jnp.float32
BF16 = jnp.bfloat16
HALF = 4
BLK = 128
ROWS = 256
HD = 128

NT = (((1,), (1,)), ((), ()))
NN = (((1,), (0,)), ((), ()))


def dot(a, b, dims):
    return lax.dot_general(a, b, dims, preferred_element_type=F32)


def head_cols(head):
    return pl.ds(pl.multiple_of(head * HD, HD), HD)


def kernel(
    seq_count,
    head_count,
    order,
    q_hbm,
    k_hbm,
    v_hbm,
    g_hbm,
    o_hbm,
    norm_ref,
    q_gain,
    k_gain,
    dq_out,
    dk_out,
    dv_out,
    q_all,
    k_all,
    g_all,
    o_all,
    q_own,
    g_own,
    k_own,
    v_own,
    k_flip,
    stats,
    q_stage,
    k_stage,
    stats_stage,
    squares,
    q_next,
    g_next,
    stats_next,
    q_far,
    g_far,
    stats_far,
    dq_acc,
    dk_acc,
    dv_acc,
    next_stage,
    next_back,
    far_stage,
    far_back,
    dq_stage,
    dk_stage,
    dv_stage,
    load_sem,
    load_g_sem,
    load_v_sem,
    sq_sem,
    xg_sem,
    xv_sem,
    xq_sem,
    xk_sem,
    xs_sem,
    ng_sem,
    nq_sem,
    ns_sem,
    fg_sem,
    fq_sem,
    fs_sem,
    nb_sem,
    fb_sem,
    od_sem,
    oq_sem,
    ok_sem,
    ov_sem,
):
    seq = lax.axis_index("seq")
    head = lax.axis_index("head")
    chip = seq // 2
    core = seq % 2
    other = 1 - core
    chips = seq_count // 2
    width = head_count * q_hbm.shape[1]
    score_scale = HD ** (-0.5)

    sibling = (chip * 2 + other, head)
    prev = (((chip + chips - 1) % chips) * 2 + core, head)
    succ = (((chip + 1) % chips) * 2 + core, head)
    prev_far = (((chip + chips - 2) % chips) * 2 + core, head)
    succ_far = (((chip + 2) % chips) * 2 + core, head)

    def remote(src, dst, sem, idx, device):
        return pltpu.make_async_remote_copy(
            src_ref=src,
            dst_ref=dst,
            send_sem=sem.at[(0, *idx)],
            recv_sem=sem.at[(1, *idx)],
            device_id=device,
            device_id_type=MESH,
        )

    loads = [
        pltpu.make_async_copy(src, dst, load_sem.at[n])
        for n, (src, dst) in enumerate(
            ((q_hbm, q_all), (k_hbm, k_all), (g_hbm, g_all), (o_hbm, o_all))
        )
    ]

    def load_g(h):
        return pltpu.make_async_copy(
            g_hbm.at[:, head_cols(core * HALF + h)], g_own.at[h, core], load_g_sem.at[h]
        )

    def load_v(h):
        return pltpu.make_async_copy(
            v_hbm.at[:, head_cols(core * HALF + h)], v_own.at[h, core], load_v_sem.at[h]
        )

    loads[0].start()
    loads[1].start()
    for h in range(HALF):
        load_g(h).start()
    loads[2].start()
    loads[3].start()
    for h in range(HALF):
        load_v(h).start()

    barrier = pltpu.get_barrier_semaphore()
    for device in (sibling, prev, succ, prev_far, succ_far):
        pl.semaphore_signal(barrier, inc=1, device_id=device, device_id_type=MESH)
    for n in range(1, head_count):
        pl.semaphore_signal(
            barrier, inc=1, device_id=(seq, (head + n) % head_count), device_id_type=MESH
        )
    pl.semaphore_wait(barrier, 5 + head_count - 1)

    def give_g(h):
        return remote(
            g_hbm.at[:, head_cols(other * HALF + h)], g_own.at[h, core], xg_sem, (h,), sibling
        )

    def give_v(h):
        return remote(
            v_hbm.at[:, head_cols(other * HALF + h)], v_own.at[h, core], xv_sem, (h,), sibling
        )

    def give_q(h):
        return remote(q_stage.at[h], q_own.at[h, core], xq_sem, (h,), sibling)

    def give_k(h):
        return remote(k_stage.at[h], k_own.at[h, core], xk_sem, (h,), sibling)

    give_s = remote(stats_stage, stats.at[core], xs_sem, (0,), sibling)

    def send_g(h, g):
        return remote(g_own.at[h, g], g_next.at[h, g], ng_sem, (h, g), prev)

    def send_q(h, g):
        return remote(q_own.at[h, g], q_next.at[h, g], nq_sem, (h, g), prev)

    send_s = remote(stats, stats_next, ns_sem, (0,), prev)

    def send_far_g(h):
        return remote(g_own.at[h, 0], g_far.at[h], fg_sem, (h,), prev_far)

    def send_far_q(h):
        return remote(q_own.at[h, 0], q_far.at[h], fq_sem, (h,), prev_far)

    send_far_s = remote(stats.at[0], stats_far, fs_sem, (0,), prev_far)

    def back_next(h, g):
        return remote(next_stage.at[h, g], next_back.at[h, g], nb_sem, (h, g), succ)

    def back_far(h):
        return remote(far_stage.at[h], far_back.at[h], fb_sem, (h,), succ_far)

    def over_heads(body):
        lax.fori_loop(0, HALF, lambda h, c: (body(h), c)[1], 0)

    over_heads(lambda h: give_g(h).start())

    def first_g(h):
        load_g(h).wait()
        send_g(h, core).start()

        @pl.when(core == 0)
        def _():
            send_far_g(h).start()

    over_heads(first_g)

    def row_sums(src):
        def add(h, total):
            block = src[:, head_cols(h)].astype(F32)
            return total + block * block

        total = lax.fori_loop(0, 2 * HALF, add, jnp.zeros((ROWS, HD), F32))
        return jnp.sum(total.T, axis=0, keepdims=True)

    loads[0].wait()
    loads[1].wait()
    squares[0] = jnp.zeros((8, ROWS), F32)
    squares[0, 0:1, :] = row_sums(q_all)
    squares[0, 1:2, :] = row_sums(k_all)
    sq_copies = []
    for n in range(1, head_count):
        copy = remote(
            squares.at[0], squares.at[n], sq_sem, (n,), (seq, (head + n) % head_count)
        )
        copy.start()
        sq_copies.append(copy)

    over_heads(lambda h: give_v(h).start())

    loads[2].wait()
    loads[3].wait()
    norm_rows = norm_ref[...] * LOG2E

    def delta_row(h):
        product = g_all[:, head_cols(h)].astype(F32) * o_all[:, head_cols(h)].astype(F32)
        return jnp.sum(product.T, axis=0, keepdims=True)

    first_half = core == 0
    stats[core, 0:HALF, :] = jnp.where(first_half, norm_rows[0:HALF], norm_rows[HALF:])
    stats_stage[0:HALF, :] = jnp.where(first_half, norm_rows[HALF:], norm_rows[0:HALF])
    for h in range(HALF):
        stats[core, HALF + h : HALF + h + 1, :] = delta_row(core * HALF + h)
        stats_stage[HALF + h : HALF + h + 1, :] = delta_row(other * HALF + h)
    give_s.start()

    def second_g(h):
        give_g(h).wait_recv()
        send_g(h, other).start()

        @pl.when(core == 1)
        def _():
            send_far_g(h).start()

    over_heads(second_g)
    give_s.wait_recv()
    send_s.start()
    send_far_s.start()

    for copy in sq_copies:
        copy.wait_recv()
    total = squares[0, 0:2, :]
    for n in range(1, head_count):
        total = total + squares[n, 0:2, :]
    scale = lax.rsqrt(total / width + EPSILON)
    q_scale = jnp.broadcast_to(scale[0:1, :], (HD, ROWS)).T
    k_scale = jnp.broadcast_to(scale[1:2, :], (HD, ROWS)).T

    def normed(src, scales, gain, h):
        return (src[:, head_cols(h)].astype(F32) * scales * gain[0:1, head_cols(h)]).astype(BF16)

    def norm_q(h):
        q_stage[h] = normed(q_all, q_scale, q_gain, other * HALF + h)
        give_q(h).start()
        q_own[h, core] = normed(q_all, q_scale, q_gain, core * HALF + h)
        send_q(h, core).start()

        @pl.when(core == 0)
        def _():
            send_far_q(h).start()

    over_heads(norm_q)

    def norm_k(h):
        k_stage[h] = normed(k_all, k_scale, k_gain, other * HALF + h)
        give_k(h).start()
        mine = normed(k_all, k_scale, k_gain, core * HALF + h)
        k_own[h, core] = mine
        k_flip[h, core] = mine.T

    over_heads(norm_k)

    def second_q(h):
        give_q(h).wait_recv()
        send_q(h, other).start()

        @pl.when(core == 1)
        def _():
            send_far_q(h).start()

    over_heads(second_q)

    def ready_kv(h):
        give_k(h).wait_recv()
        k_flip[h, other] = k_own[h, other].T
        give_v(h).wait_recv()
        load_v(h).wait()

    over_heads(ready_kv)

    def group_of(step):
        return (chip * 2 + step) % seq_count

    def key_pos(c):
        group = group_of(c)
        row = lax.broadcasted_iota(jnp.int32, (ROWS, ROWS), 0)
        return row + jnp.where(row < BLK, order[2 * group] * BLK, order[2 * group + 1] * BLK - BLK)

    def query_pos(step):
        group = group_of(step)
        col = lax.broadcasted_iota(jnp.int32, (1, ROWS), 1)
        return col + jnp.where(col < BLK, order[2 * group] * BLK, order[2 * group + 1] * BLK - BLK)

    def pair(h, c, q, g, norm_row, delta, q_at):
        s = dot(k_own[h, c], q, NT)
        d = dot(v_own[h, c], g, NT)
        p = jnp.exp2(s * (score_scale * LOG2E) - norm_row)
        p = jnp.where(key_pos(c) <= q_at, p, 0.0)
        ds = (p * (d - delta)).astype(BF16)
        dv_add = dot(p.astype(BF16), g, NN)
        dk_add = dot(ds, q, NN)
        dq_add = dot(k_flip[h, c], ds, NN)
        return dq_add, dk_add, dv_add

    def out_copy(stage, out, sem, n, h):
        mine = pltpu.make_async_copy(
            stage.at[h, core], out.at[:, head_cols(core * HALF + h)], od_sem.at[n, h]
        )
        theirs = remote(
            stage.at[h, other], out.at[:, head_cols(core * HALF + h)], sem, (h,), sibling
        )
        return mine, theirs

    def out_start(stage, out, sem, n, h):
        for copy in out_copy(stage, out, sem, n, h):
            copy.start()

    def out_wait(stage, out, sem, n, h):
        for copy in out_copy(stage, out, sem, n, h):
            copy.wait()

    def step(h):
        norm_of = lambda ref, g: ref[g, pl.ds(h, 1), :]
        delta_of = lambda ref, g: ref[g, pl.ds(HALF + h, 1), :]
        q0, g0, q1, g1 = q_own[h, 0], g_own[h, 0], q_own[h, 1], g_own[h, 1]
        n0, d0 = norm_of(stats, 0), delta_of(stats, 0)
        n1, d1 = norm_of(stats, 1), delta_of(stats, 1)
        dq_add, dk_add, dv_add = pair(h, 0, q0, g0, n0, d0, query_pos(0))
        dq_acc[h, 0] = dq_add
        dk_acc[0] = dk_add
        dv_acc[0] = dv_add
        dq_add, dk_add, dv_add = pair(h, 0, q1, g1, n1, d1, query_pos(1))
        dq_acc[h, 1] = dq_add
        dk_acc[0] += dk_add
        dv_acc[0] += dv_add
        dq_add, dk_add, dv_add = pair(h, 1, q1, g1, n1, d1, query_pos(1))
        dq_acc[h, 1] += dq_add
        dk_acc[1] = dk_add
        dv_acc[1] = dv_add

        @pl.when(h == 0)
        def _():
            send_far_s.wait_recv()
            send_s.wait_recv()

        send_far_g(h).wait_recv()
        send_far_q(h).wait_recv()
        dq_add, dk_add, dv_add = pair(
            h,
            1,
            q_far[h],
            g_far[h],
            stats_far[pl.ds(h, 1), :],
            stats_far[pl.ds(HALF + h, 1), :],
            query_pos(4),
        )
        far_stage[h] = dq_add.astype(BF16)
        back_far(h).start()
        dk_acc[1] += dk_add
        dv_acc[1] += dv_add

        for g in range(2):
            send_g(h, g).wait_recv()
            send_q(h, g).wait_recv()
            qn, gn = q_next[h, g], g_next[h, g]
            nn, dn = norm_of(stats_next, g), delta_of(stats_next, g)
            first, dk_add, dv_add = pair(h, 0, qn, gn, nn, dn, query_pos(2 + g))
            dk_acc[0] += dk_add
            dv_acc[0] += dv_add
            second, dk_add, dv_add = pair(h, 1, qn, gn, nn, dn, query_pos(2 + g))
            dk_acc[1] += dk_add
            dv_acc[1] += dv_add
            next_stage[h, g] = (first + second).astype(BF16)
            back_next(h, g).start()

        for c in range(2):
            dk_stage[h, c] = (dk_acc[c] * score_scale).astype(BF16)
            dv_stage[h, c] = dv_acc[c].astype(BF16)
        out_start(dk_stage, dk_out, ok_sem, 0, h)
        out_start(dv_stage, dv_out, ov_sem, 1, h)

    over_heads(step)

    def finish(h):
        back_far(h).wait_recv()
        for g in range(2):
            back_next(h, g).wait_recv()
            total = dq_acc[h, g] + next_back[h, g].astype(F32)
            if g == 0:
                total = total + far_back[h].astype(F32)
            dq_stage[h, g] = (total * score_scale).T.astype(BF16)
        out_start(dq_stage, dq_out, oq_sem, 2, h)

    over_heads(finish)

    for copy in sq_copies:
        copy.wait_send()
    give_s.wait_send()
    send_s.wait_send()
    send_far_s.wait_send()

    def drain(h):
        give_g(h).wait_send()
        give_v(h).wait_send()
        give_q(h).wait_send()
        give_k(h).wait_send()
        for g in range(2):
            send_g(h, g).wait_send()
            send_q(h, g).wait_send()
            back_next(h, g).wait_send()
        send_far_g(h).wait_send()
        send_far_q(h).wait_send()
        back_far(h).wait_send()
        out_wait(dk_stage, dk_out, ok_sem, 0, h)
        out_wait(dv_stage, dv_out, ov_sem, 1, h)
        out_wait(dq_stage, dq_out, oq_sem, 2, h)

    over_heads(drain)


def local(q_raw, k_raw, values, out_grad, attn_out, log_norm, q_gain, k_gain, order):
    seq_count = lax.axis_size("seq")
    head_count = lax.axis_size("head")
    rows, columns = q_raw.shape
    any_spec = pl.BlockSpec(memory_space=pl.ANY)
    vmem_spec = pl.BlockSpec(memory_space=pltpu.VMEM)
    whole = pltpu.VMEM((rows, columns), BF16)
    halves = pltpu.VMEM((HALF, 2, ROWS, HD), BF16)
    single = pltpu.VMEM((HALF, ROWS, HD), BF16)
    flipped = pltpu.VMEM((HALF, 2, HD, ROWS), BF16)
    table = pltpu.VMEM((2, 2 * HALF, ROWS), F32)
    table_one = pltpu.VMEM((2 * HALF, ROWS), F32)
    acc = pltpu.VMEM((2, ROWS, HD), F32)
    sem = pltpu.SemaphoreType.DMA
    scratch = [whole] * 4
    scratch += [halves, halves, halves, halves, flipped, table]
    scratch += [single, single, table_one]
    scratch += [pltpu.VMEM((head_count, 8, ROWS), F32)]
    scratch += [halves, halves, table, single, single, table_one]
    scratch += [pltpu.VMEM((HALF, 2, HD, ROWS), F32), acc, acc]
    scratch += [flipped, flipped]
    scratch += [pltpu.VMEM((HALF, HD, ROWS), BF16), pltpu.VMEM((HALF, HD, ROWS), BF16)]
    scratch += [halves, halves, halves]
    scratch += [sem((4,)), sem((HALF,)), sem((HALF,)), sem((2, head_count))]
    scratch += [sem((2, HALF))] * 4 + [sem((2, 1))]
    scratch += [sem((2, HALF, 2))] * 2 + [sem((2, 1))]
    scratch += [sem((2, HALF))] * 2 + [sem((2, 1))]
    scratch += [sem((2, HALF, 2)), sem((2, HALF))]
    scratch += [sem((3, HALF))] + [sem((2, HALF))] * 3
    shape = jax.ShapeDtypeStruct((rows, columns), BF16)
    return pl.pallas_call(
        functools.partial(kernel, seq_count, head_count),
        out_shape=(shape, shape, shape),
        in_specs=[pl.BlockSpec(memory_space=pltpu.SMEM)] + [any_spec] * 5 + [vmem_spec] * 3,
        out_specs=(any_spec, any_spec, any_spec),
        scratch_shapes=scratch,
        compiler_params=pltpu.CompilerParams(
            collective_id=0, has_side_effects=True, vmem_limit_bytes=62 * 1024 * 1024
        ),
        cost_estimate=pl.CostEstimate(
            flops=10 * 32 * ROWS * ROWS * HD,
            bytes_accessed=8 * rows * columns * 2,
            transcendentals=32 * ROWS * ROWS,
        ),
    )(
        order,
        q_raw,
        k_raw,
        values,
        out_grad,
        attn_out,
        log_norm,
        q_gain.reshape(1, columns),
        k_gain.reshape(1, columns),
    )


def solution(mesh):
    placed = P("seq", "head")
    return jax.shard_map(
        local,
        mesh=mesh,
        in_specs=(placed,) * 5 + (P("head", "seq"), P("head"), P("head"), P()),
        out_specs=(placed, placed, placed),
        check_vma=False,
    )
```

time: 184 us -> 66.8 us (0.36); the launches traced: 181 us -> 66.6 us
  waiting for transfers between devices: 63.1 us -> 0 us
  Pallas kernels: 0 us -> 62 us
  starting transfers between devices: 37.2 us -> 0 us
  matrix products: 33.5 us -> 0 us
  blocking collectives: 16.8 us -> 0 us
  local copies, waits for them, and re-layouts: 20.6 us -> 3.95 us
  other arithmetic: 8.16 us -> 0 us
    ppermute x14 -> x0, waiting for transfers between devices: 63.1 us -> none  [passed_along(): lax.ppermute(value, axis, [(i, (i + by) % peers) for i in range(peers)])]
    pallas_call x0 -> x1, Pallas kernels: none -> 62 us  [local(): pl.pallas_call(functools.partial(kernel, seq_count, head_count), out_shap...]
    ppermute x14 -> x0, starting transfers between devices: 37.2 us -> none  [passed_along(): lax.ppermute(value, axis, [(i, (i + by) % peers) for i in range(peers)])]
    dot_general x80 -> x0, matrix products: 33.5 us -> none  [the longest x16 9.15 us: pair_terms(): jnp.einsum('qhd,khd->hqk', query_block, key_block, preferred_element_type...]
    psum x1 -> x0, blocking collectives: 16.8 us -> none  [local(): lax.psum((jnp.sum(query_wide * query_wide, axis=1), jnp.sum(key_wide * ke...]
    unnamed x49 -> x7, local copies, waits for them, and re-layouts: 15.6 us -> 3.95 us
    reshape x3 -> x0, local copies, waits for them, and re-layouts: 3.08 us -> none  [the longest x2 2.98 us: local(): key_pair = key_normed.reshape(shape_four)]
    reduce_sum x3 -> x0, other arithmetic: 1.97 us -> none  [the longest x1 1.63 us: local(): jnp.sum(products.reshape(tok_rows, head_count, head_dim), axis=2)]
  transfers between devices with their start and end apart: 14 -> 0, of which waited for: 6 -> 0; matrix products, arithmetic and copies ran while one was open for 26% -> 0% of each run, Pallas kernels for 0% -> 0%
where the time goes in v1:
time: 66.8 us; the launch traced here: 66.6 us
  Pallas kernels  62 us (93%)
  local copies, waits for them, and re-layouts  3.95 us (6%)
    pallas_call x1, Pallas kernels, local(): pl.pallas_call(functools.partial(kernel, seq_count, head_count), out_shap...  62 us
    unnamed x7, local copies, waits for them, and re-layouts  3.95 us

profile of v1, /device:TPU:1, one launch (start us, length us, event | category | flops | bytes accessed | tf_op | source)
XLA Modules:
  0.0 66.6 jit_solution(14182210435055208623)
XLA Ops:
  0.6 62.0 %shard_map.112 = (bf16[256,1024]{1,0:T(8,128)(2,1)}, bf16[256,1024]{1,0:T(8,128)(2,1)}, bf16[256,1024]{1,0:T(8,128)(2,1)}) custom-call(s32[64]{0:T(128)} %order.1, bf16[256,1024]{1,0:T(8,128)(2,1)} %q_hbm.1, bf16[256,1024]{1,0:T(8,128)(2,1)} %k_hbm.1, bf16[256,1024]{1,0:T(8,128)(2,1)} %v_hbm.1, bf16[256,1024]{1,0:T(8,128)(2,1)} %g_hbm.1, ...), custom_call_target="tpu_custom_call" | custom-call | flops 2684354560 | bytes 4194304 | tf_op jit(solution)/shard_map/pallas_call | solution.py:487
  62.6 0.0 copy-start.1
  62.6 1.9 %copy.15 = bf16[256,1024]{1,0:T(8,128)(2,1)} copy(bf16[256,1024]{1,0:T(8,128)(2,1)} %get-tuple-element.6) | data formatting | bytes 1048576
  64.6 0.0 copy-done.1
  64.6 0.0 copy-start
  64.6 0.8 %copy.16 = bf16[256,1024]{1,0:T(8,128)(2,1)} copy(bf16[256,1024]{1,0:T(8,128)(2,1)S(1)} %copy-done.1) | data formatting | bytes 1048576
  65.4 0.4 copy-done
  65.8 0.8 %copy.17 = bf16[256,1024]{1,0:T(8,128)(2,1)} copy(bf16[256,1024]{1,0:T(8,128)(2,1)S(1)} %copy-done) | data formatting | bytes 1048576
Async XLA Ops:
  62.6 1.9 %copy-start.1 = (bf16[256,1024]{1,0:T(8,128)(2,1)S(1)}, bf16[256,1024]{1,0:T(8,128)(2,1)}, u32[]{:S(2)}) copy-start(bf16[256,1024]{1,0:T(8,128)(2,1)} %get-tuple-element.7) | copy-start | bytes 1572868
  64.6 1.2 %copy-start = (bf16[256,1024]{1,0:T(8,128)(2,1)S(1)}, bf16[256,1024]{1,0:T(8,128)(2,1)}, u32[]{:S(2)}) copy-start(bf16[256,1024]{1,0:T(8,128)(2,1)} %get-tuple-element.8) | copy-start | bytes 1572868

commit v2 on v1

--- a/solution.py
+++ b/solution.py
@@ -121,6 +121,14 @@
             device_id_type=MESH,
         )
 
+    barrier = pltpu.get_barrier_semaphore()
+    for device in (sibling, prev, succ, prev_far, succ_far):
+        pl.semaphore_signal(barrier, inc=1, device_id=device, device_id_type=MESH)
+    for n in range(1, head_count):
+        pl.semaphore_signal(
+            barrier, inc=1, device_id=(seq, (head + n) % head_count), device_id_type=MESH
+        )
+
     loads = [
         pltpu.make_async_copy(src, dst, load_sem.at[n])
         for n, (src, dst) in enumerate(
@@ -147,70 +155,6 @@
     for h in range(HALF):
         load_v(h).start()
 
-    barrier = pltpu.get_barrier_semaphore()
-    for device in (sibling, prev, succ, prev_far, succ_far):
-        pl.semaphore_signal(barrier, inc=1, device_id=device, device_id_type=MESH)
-    for n in range(1, head_count):
-        pl.semaphore_signal(
-            barrier, inc=1, device_id=(seq, (head + n) % head_count), device_id_type=MESH
-        )
-    pl.semaphore_wait(barrier, 5 + head_count - 1)
-
-    def give_g(h):
-        return remote(
-            g_hbm.at[:, head_cols(other * HALF + h)], g_own.at[h, core], xg_sem, (h,), sibling
-        )
-
-    def give_v(h):
-        return remote(
-            v_hbm.at[:, head_cols(other * HALF + h)], v_own.at[h, core], xv_sem, (h,), sibling
-        )
-
-    def give_q(h):
-        return remote(q_stage.at[h], q_own.at[h, core], xq_sem, (h,), sibling)
-
-    def give_k(h):
-        return remote(k_stage.at[h], k_own.at[h, core], xk_sem, (h,), sibling)
-
-    give_s = remote(stats_stage, stats.at[core], xs_sem, (0,), sibling)
-
-    def send_g(h, g):
-        return remote(g_own.at[h, g], g_next.at[h, g], ng_sem, (h, g), prev)
-
-    def send_q(h, g):
-        return remote(q_own.at[h, g], q_next.at[h, g], nq_sem, (h, g), prev)
-
-    send_s = remote(stats, stats_next, ns_sem, (0,), prev)
-
-    def send_far_g(h):
-        return remote(g_own.at[h, 0], g_far.at[h], fg_sem, (h,), prev_far)
-
-    def send_far_q(h):
-        return remote(q_own.at[h, 0], q_far.at[h], fq_sem, (h,), prev_far)
-
-    send_far_s = remote(stats.at[0], stats_far, fs_sem, (0,), prev_far)
-
-    def back_next(h, g):
-        return remote(next_stage.at[h, g], next_back.at[h, g], nb_sem, (h, g), succ)
-
-    def back_far(h):
-        return remote(far_stage.at[h], far_back.at[h], fb_sem, (h,), succ_far)
-
-    def over_heads(body):
-        lax.fori_loop(0, HALF, lambda h, c: (body(h), c)[1], 0)
-
-    over_heads(lambda h: give_g(h).start())
-
-    def first_g(h):
-        load_g(h).wait()
-        send_g(h, core).start()
-
-        @pl.when(core == 0)
-        def _():
-            send_far_g(h).start()
-
-    over_heads(first_g)
-
     def row_sums(src):
         def add(h, total):
             block = src[:, head_cols(h)].astype(F32)
@@ -221,9 +165,68 @@
 
     loads[0].wait()
     loads[1].wait()
-    squares[0] = jnp.zeros((8, ROWS), F32)
     squares[0, 0:1, :] = row_sums(q_all)
     squares[0, 1:2, :] = row_sums(k_all)
+    pl.semaphore_wait(barrier, 5 + head_count - 1)
+
+    def give_g(h):
+        return remote(
+            g_hbm.at[:, head_cols(other * HALF + h)], g_own.at[h, core], xg_sem, (h,), sibling
+        )
+
+    def give_v(h):
+        return remote(
+            v_hbm.at[:, head_cols(other * HALF + h)], v_own.at[h, core], xv_sem, (h,), sibling
+        )
+
+    def give_q(h):
+        return remote(q_stage.at[h], q_own.at[h, core], xq_sem, (h,), sibling)
+
+    def give_k(h):
+        return remote(k_stage.at[h], k_own.at[h, core], xk_sem, (h,), sibling)
+
+    give_s = remote(stats_stage, stats.at[core], xs_sem, (0,), sibling)
+
+    def send_g(h, g):
+        return remote(g_own.at[h, g], g_next.at[h, g], ng_sem, (h, g), prev)
+
+    def send_q(h, g):
+        return remote(q_own.at[h, g], q_next.at[h, g], nq_sem, (h, g), prev)
+
+    send_s = remote(stats, stats_next, ns_sem, (0,), prev)
+
+    def send_far_g(h):
+        return remote(g_own.at[h, 0], g_far.at[h], fg_sem, (h,), prev_far)
+
+    def send_far_q(h):
+        return remote(q_own.at[h, 0], q_far.at[h], fq_sem, (h,), prev_far)
+
+    send_far_s = remote(stats.at[0], stats_far, fs_sem, (0,), prev_far)
+
+    def back_next(h, g):
+        return remote(next_stage.at[h, g], next_back.at[h, g], nb_sem, (h, g), succ)
+
+    def back_far(h):
+        return remote(far_stage.at[h], far_back.at[h], fb_sem, (h,), succ_far)
+
+    def over_heads(body, first=0, last=HALF):
+        lax.fori_loop(first, last, lambda h, c: (body(h), c)[1], 0)
+
+    def start_next(send, h, g):
+        @pl.when(g + chip % 2 > 0)
+        def _():
+            send(h, g).start()
+
+    def start_far(send, h, g):
+        @pl.when(g == 0)
+        def _():
+            send(h).start()
+
+    def pass_on(src, dst, sem, h):
+        @pl.when(chip % 2 == 0)
+        def _():
+            remote(src.at[h], dst.at[h, 0], sem, (h, 0), succ).start()
+
     sq_copies = []
     for n in range(1, head_count):
         copy = remote(
@@ -232,6 +235,14 @@
         copy.start()
         sq_copies.append(copy)
 
+    over_heads(lambda h: give_g(h).start())
+
+    def first_g(h):
+        load_g(h).wait()
+        start_far(send_far_g, h, core)
+        start_next(send_g, h, core)
+
+    over_heads(first_g)
     over_heads(lambda h: give_v(h).start())
 
     loads[2].wait()
@@ -252,22 +263,20 @@
 
     def second_g(h):
         give_g(h).wait_recv()
-        send_g(h, other).start()
-
-        @pl.when(core == 1)
-        def _():
-            send_far_g(h).start()
-
-    over_heads(second_g)
+        start_far(send_far_g, h, other)
+        start_next(send_g, h, other)
+
+    over_heads(second_g, 0, HALF // 2)
+
+    for copy in sq_copies:
+        copy.wait_recv()
+    over_heads(second_g, HALF // 2)
     give_s.wait_recv()
     send_s.start()
     send_far_s.start()
-
-    for copy in sq_copies:
-        copy.wait_recv()
-    total = squares[0, 0:2, :]
+    total = squares[0]
     for n in range(1, head_count):
-        total = total + squares[n, 0:2, :]
+        total = total + squares[n]
     scale = lax.rsqrt(total / width + EPSILON)
     q_scale = jnp.broadcast_to(scale[0:1, :], (HD, ROWS)).T
     k_scale = jnp.broadcast_to(scale[1:2, :], (HD, ROWS)).T
@@ -279,13 +288,25 @@
         q_stage[h] = normed(q_all, q_scale, q_gain, other * HALF + h)
         give_q(h).start()
         q_own[h, core] = normed(q_all, q_scale, q_gain, core * HALF + h)
-        send_q(h, core).start()
-
-        @pl.when(core == 0)
-        def _():
-            send_far_q(h).start()
 
     over_heads(norm_q)
+
+    def queue_q(h):
+        start_far(send_far_q, h, core)
+        start_next(send_q, h, core)
+        give_q(h).wait_recv()
+        start_far(send_far_q, h, other)
+        start_next(send_q, h, other)
+
+    over_heads(queue_q)
+
+    def pass_g(h):
+        send_far_g(h).wait_recv()
+        pass_on(g_far, g_next, ng_sem, h)
+
+    @pl.when(core == 0)
+    def _():
+        over_heads(pass_g)
 
     def norm_k(h):
         k_stage[h] = normed(k_all, k_scale, k_gain, other * HALF + h)
@@ -295,16 +316,6 @@
         k_flip[h, core] = mine.T
 
     over_heads(norm_k)
-
-    def second_q(h):
-        give_q(h).wait_recv()
-        send_q(h, other).start()
-
-        @pl.when(core == 1)
-        def _():
-            send_far_q(h).start()
-
-    over_heads(second_q)
 
     def ready_kv(h):
         give_k(h).wait_recv()
@@ -355,32 +366,38 @@
         for copy in out_copy(stage, out, sem, n, h):
             copy.wait()
 
-    def step(h):
-        norm_of = lambda ref, g: ref[g, pl.ds(h, 1), :]
-        delta_of = lambda ref, g: ref[g, pl.ds(HALF + h, 1), :]
+    norm_of = lambda ref, g, h: ref[g, pl.ds(h, 1), :]
+    delta_of = lambda ref, g, h: ref[g, pl.ds(HALF + h, 1), :]
+
+    def own(h):
         q0, g0, q1, g1 = q_own[h, 0], g_own[h, 0], q_own[h, 1], g_own[h, 1]
-        n0, d0 = norm_of(stats, 0), delta_of(stats, 0)
-        n1, d1 = norm_of(stats, 1), delta_of(stats, 1)
+        n0, d0 = norm_of(stats, 0, h), delta_of(stats, 0, h)
+        n1, d1 = norm_of(stats, 1, h), delta_of(stats, 1, h)
         dq_add, dk_add, dv_add = pair(h, 0, q0, g0, n0, d0, query_pos(0))
         dq_acc[h, 0] = dq_add
-        dk_acc[0] = dk_add
-        dv_acc[0] = dv_add
+        dk_acc[h, 0] = dk_add
+        dv_acc[h, 0] = dv_add
         dq_add, dk_add, dv_add = pair(h, 0, q1, g1, n1, d1, query_pos(1))
         dq_acc[h, 1] = dq_add
-        dk_acc[0] += dk_add
-        dv_acc[0] += dv_add
+        dk_acc[h, 0] += dk_add
+        dv_acc[h, 0] += dv_add
         dq_add, dk_add, dv_add = pair(h, 1, q1, g1, n1, d1, query_pos(1))
         dq_acc[h, 1] += dq_add
-        dk_acc[1] = dk_add
-        dv_acc[1] = dv_add
-
-        @pl.when(h == 0)
+        dk_acc[h, 1] = dk_add
+        dv_acc[h, 1] = dv_add
+
+        @pl.when(core == 1)
         def _():
-            send_far_s.wait_recv()
-            send_s.wait_recv()
-
-        send_far_g(h).wait_recv()
+            pass_g(h)
+
+    over_heads(own)
+
+    send_far_s.wait_recv()
+    send_s.wait_recv()
+
+    def step(h):
         send_far_q(h).wait_recv()
+        pass_on(q_far, q_next, nq_sem, h)
         dq_add, dk_add, dv_add = pair(
             h,
             1,
@@ -392,26 +409,26 @@
         )
         far_stage[h] = dq_add.astype(BF16)
         back_far(h).start()
-        dk_acc[1] += dk_add
-        dv_acc[1] += dv_add
-
-        for g in range(2):
+        dk_acc[h, 1] += dk_add
+        dv_acc[h, 1] += dv_add
+
+        for g in (1, 0):
             send_g(h, g).wait_recv()
             send_q(h, g).wait_recv()
             qn, gn = q_next[h, g], g_next[h, g]
-            nn, dn = norm_of(stats_next, g), delta_of(stats_next, g)
+            nn, dn = norm_of(stats_next, g, h), delta_of(stats_next, g, h)
             first, dk_add, dv_add = pair(h, 0, qn, gn, nn, dn, query_pos(2 + g))
-            dk_acc[0] += dk_add
-            dv_acc[0] += dv_add
+            dk_acc[h, 0] += dk_add
+            dv_acc[h, 0] += dv_add
             second, dk_add, dv_add = pair(h, 1, qn, gn, nn, dn, query_pos(2 + g))
-            dk_acc[1] += dk_add
-            dv_acc[1] += dv_add
+            dk_acc[h, 1] += dk_add
+            dv_acc[h, 1] += dv_add
             next_stage[h, g] = (first + second).astype(BF16)
             back_next(h, g).start()
 
         for c in range(2):
-            dk_stage[h, c] = (dk_acc[c] * score_scale).astype(BF16)
-            dv_stage[h, c] = dv_acc[c].astype(BF16)
+            dk_stage[h, c] = (dk_acc[h, c] * score_scale).astype(BF16)
+            dv_stage[h, c] = dv_acc[h, c].astype(BF16)
         out_start(dk_stage, dk_out, ok_sem, 0, h)
         out_start(dv_stage, dv_out, ov_sem, 1, h)
 
@@ -419,7 +436,7 @@
 
     def finish(h):
         back_far(h).wait_recv()
-        for g in range(2):
+        for g in (1, 0):
             back_next(h, g).wait_recv()
             total = dq_acc[h, g] + next_back[h, g].astype(F32)
             if g == 0:
@@ -454,6 +471,41 @@
     over_heads(drain)
 
 
+def store_kernel(*refs):
+    ins, outs, (held, sem_in, sem_out) = refs[:3], refs[3:6], refs[6:]
+    half = ROWS // 2
+    parts = [(n, part) for n in range(3) for part in range(2)]
+
+    def load(n, part):
+        rows = pl.ds(part * half, half)
+        return pltpu.make_async_copy(ins[n].at[rows], held.at[n, rows], sem_in.at[n, part])
+
+    def save(n, part):
+        rows = pl.ds(part * half, half)
+        return pltpu.make_async_copy(held.at[n, rows], outs[n].at[rows], sem_out.at[n, part])
+
+    for n, part in parts:
+        load(n, part).start()
+    for n, part in parts:
+        load(n, part).wait()
+        save(n, part).start()
+    for n, part in parts:
+        save(n, part).wait()
+
+
+def store(grads, shape):
+    any_spec = pl.BlockSpec(memory_space=pl.ANY)
+    sem = pltpu.SemaphoreType.DMA
+    return pl.pallas_call(
+        store_kernel,
+        out_shape=(shape,) * 3,
+        in_specs=[any_spec] * 3,
+        out_specs=(any_spec,) * 3,
+        scratch_shapes=[pltpu.VMEM((3, *shape.shape), BF16), sem((3, 2)), sem((3, 2))],
+        compiler_params=pltpu.CompilerParams(vmem_limit_bytes=62 * 1024 * 1024),
+    )(*grads)
+
+
 def local(q_raw, k_raw, values, out_grad, attn_out, log_norm, q_gain, k_gain, order):
     seq_count = lax.axis_size("seq")
     head_count = lax.axis_size("head")
@@ -466,12 +518,12 @@
     flipped = pltpu.VMEM((HALF, 2, HD, ROWS), BF16)
     table = pltpu.VMEM((2, 2 * HALF, ROWS), F32)
     table_one = pltpu.VMEM((2 * HALF, ROWS), F32)
-    acc = pltpu.VMEM((2, ROWS, HD), F32)
+    acc = pltpu.VMEM((HALF, 2, ROWS, HD), F32)
     sem = pltpu.SemaphoreType.DMA
     scratch = [whole] * 4
     scratch += [halves, halves, halves, halves, flipped, table]
     scratch += [single, single, table_one]
-    scratch += [pltpu.VMEM((head_count, 8, ROWS), F32)]
+    scratch += [pltpu.VMEM((head_count, 2, ROWS), F32)]
     scratch += [halves, halves, table, single, single, table_one]
     scratch += [pltpu.VMEM((HALF, 2, HD, ROWS), F32), acc, acc]
     scratch += [flipped, flipped]
@@ -484,7 +536,7 @@
     scratch += [sem((2, HALF, 2)), sem((2, HALF))]
     scratch += [sem((3, HALF))] + [sem((2, HALF))] * 3
     shape = jax.ShapeDtypeStruct((rows, columns), BF16)
-    return pl.pallas_call(
+    grads = pl.pallas_call(
         functools.partial(kernel, seq_count, head_count),
         out_shape=(shape, shape, shape),
         in_specs=[pl.BlockSpec(memory_space=pltpu.SMEM)] + [any_spec] * 5 + [vmem_spec] * 3,
@@ -509,6 +561,7 @@
         q_gain.reshape(1, columns),
         k_gain.reshape(1, columns),
     )
+    return store(grads, shape)
 
 
 def solution(mesh):

time: 66.8 us -> 59.9 us (0.90)
  local copies, waits for them, and re-layouts: 3.95 us -> 0 us
  Pallas kernels: 62 us -> 59.1 us
    pallas_call x1, Pallas kernels: 62 us -> 56.9 us  [local(): pl.pallas_call(functools.partial(kernel, seq_count, head_count), out_shap...]
    unnamed x7 -> x0, local copies, waits for them, and re-layouts: 3.95 us -> none
    pallas_call x0 -> x1, Pallas kernels: none -> 2.19 us  [store(): pl.pallas_call(store_kernel, out_shape=(shape,) * 3, in_specs=[any_spec]...]
where the time goes in v2:
time: 59.9 us; the launch traced here: 59.7 us
  Pallas kernels  59.1 us (99%)
  between operations  0.64 us (1%)
    pallas_call x1, Pallas kernels, local(): pl.pallas_call(functools.partial(kernel, seq_count, head_count), out_shap...  56.9 us
    pallas_call x1, Pallas kernels, store(): pl.pallas_call(store_kernel, out_shape=(shape,) * 3, in_specs=[any_spec]...  2.19 us

profile of v2, /device:TPU:1, one launch (start us, length us, event | category | flops | bytes accessed | tf_op | source)
XLA Modules:
  0.0 59.7 jit_solution(15508779516352012299)
XLA Ops:
  0.6 56.9 %shard_map.112 = (bf16[256,1024]{1,0:T(8,128)(2,1)}, bf16[256,1024]{1,0:T(8,128)(2,1)}, bf16[256,1024]{1,0:T(8,128)(2,1)}) custom-call(s32[64]{0:T(128)} %order.1, bf16[256,1024]{1,0:T(8,128)(2,1)} %q_hbm.1, bf16[256,1024]{1,0:T(8,128)(2,1)} %k_hbm.1, bf16[256,1024]{1,0:T(8,128)(2,1)} %v_hbm.1, bf16[256,1024]{1,0:T(8,128)(2,1)} %g_hbm.1, ...), custom_call_target="tpu_custom_call" | custom-call | flops 2684354560 | bytes 4194304 | tf_op jit(solution)/shard_map/pallas_call | solution.py:539
  57.5 2.2 %shard_map.113 = (bf16[256,1024]{1,0:T(8,128)(2,1)}, bf16[256,1024]{1,0:T(8,128)(2,1)}, bf16[256,1024]{1,0:T(8,128)(2,1)}) custom-call(bf16[256,1024]{1,0:T(8,128)(2,1)} %get-tuple-element.6.refs_0_, bf16[256,1024]{1,0:T(8,128)(2,1)} %get-tuple-element.7.refs_1_, bf16[256,1024]{1,0:T(8,128)(2,1)} %get-tuple-element.8.refs_2_), custom_call_target="tpu_custom_call" | custom-call | tf_op jit(solution)/shard_map/pallas_call | solution.py:499

commit v3 on v2

--- a/solution.py
+++ b/solution.py
@@ -71,7 +71,7 @@
     next_back,
     far_stage,
     far_back,
-    dq_stage,
+    dq_given,
     dk_stage,
     dv_stage,
     load_sem,
@@ -91,7 +91,6 @@
     fs_sem,
     nb_sem,
     fb_sem,
-    od_sem,
     oq_sem,
     ok_sem,
     ov_sem,
@@ -111,23 +110,34 @@
     prev_far = (((chip + chips - 2) % chips) * 2 + core, head)
     succ_far = (((chip + 2) % chips) * 2 + core, head)
 
-    def remote(src, dst, sem, idx, device):
+    def on_core(device, which):
+        return (device[0] // 2 * 2 + which, head)
+
+    def remote(src, dst, sem, idx, device, there=None):
         return pltpu.make_async_remote_copy(
             src_ref=src,
             dst_ref=dst,
             send_sem=sem.at[(0, *idx)],
-            recv_sem=sem.at[(1, *idx)],
+            recv_sem=sem.at[(1, *(there or idx))],
             device_id=device,
             device_id_type=MESH,
         )
 
     barrier = pltpu.get_barrier_semaphore()
-    for device in (sibling, prev, succ, prev_far, succ_far):
-        pl.semaphore_signal(barrier, inc=1, device_id=device, device_id_type=MESH)
+
+    def signal(sem, device):
+        pl.semaphore_signal(sem, inc=1, device_id=device, device_id_type=MESH)
+
+    for device in (sibling, succ, succ_far, on_core(prev, 0), on_core(prev, 1)):
+        signal(barrier, device)
+
+    @pl.when(core == 0)
+    def _():
+        signal(barrier, on_core(prev_far, 0))
+        signal(barrier, on_core(prev_far, 1))
+
     for n in range(1, head_count):
-        pl.semaphore_signal(
-            barrier, inc=1, device_id=(seq, (head + n) % head_count), device_id_type=MESH
-        )
+        signal(barrier, (seq, (head + n) % head_count))
 
     loads = [
         pltpu.make_async_copy(src, dst, load_sem.at[n])
@@ -167,7 +177,7 @@
     loads[1].wait()
     squares[0, 0:1, :] = row_sums(q_all)
     squares[0, 1:2, :] = row_sums(k_all)
-    pl.semaphore_wait(barrier, 5 + head_count - 1)
+    pl.semaphore_wait(barrier, 6 + head_count - 1)
 
     def give_g(h):
         return remote(
@@ -204,10 +214,25 @@
     send_far_s = remote(stats.at[0], stats_far, fs_sem, (0,), prev_far)
 
     def back_next(h, g):
-        return remote(next_stage.at[h, g], next_back.at[h, g], nb_sem, (h, g), succ)
+        return remote(
+            next_stage.at[h, g], next_back.at[h, core], nb_sem, (h, g), on_core(succ, g), (h, core)
+        )
 
     def back_far(h):
-        return remote(far_stage.at[h], far_back.at[h], fb_sem, (h,), succ_far)
+        return remote(
+            far_stage.at[h], far_back.at[h, core], fb_sem, (h, 0), on_core(succ_far, 0), (h, core)
+        )
+
+    def back_next_from(h, half):
+        return remote(
+            next_stage.at[h, 0], next_back.at[h, half], nb_sem, (h, 0), sibling, (h, half)
+        )
+
+    def back_far_from(h, half):
+        return remote(far_stage.at[h], far_back.at[h, half], fb_sem, (h, 0), sibling, (h, half))
+
+    def give_dq(h):
+        return remote(dq_acc.at[h, other], dq_given.at[h], oq_sem, (h,), sibling)
 
     def over_heads(body, first=0, last=HALF):
         lax.fori_loop(first, last, lambda h, c: (body(h), c)[1], 0)
@@ -227,6 +252,13 @@
         def _():
             remote(src.at[h], dst.at[h, 0], sem, (h, 0), succ).start()
 
+    over_heads(lambda h: give_g(h).start())
+
+    def first_g(h):
+        load_g(h).wait()
+        start_next(send_g, h, core)
+
+
     sq_copies = []
     for n in range(1, head_count):
         copy = remote(
@@ -235,15 +267,15 @@
         copy.start()
         sq_copies.append(copy)
 
-    over_heads(lambda h: give_g(h).start())
-
-    def first_g(h):
-        load_g(h).wait()
-        start_far(send_far_g, h, core)
-        start_next(send_g, h, core)
-
     over_heads(first_g)
     over_heads(lambda h: give_v(h).start())
+
+    def second_g(h):
+        give_g(h).wait_recv()
+        start_next(send_g, h, other)
+
+    over_heads(second_g)
+    over_heads(lambda h: send_far_g(h).start())
 
     loads[2].wait()
     loads[3].wait()
@@ -261,16 +293,8 @@
         stats_stage[HALF + h : HALF + h + 1, :] = delta_row(other * HALF + h)
     give_s.start()
 
-    def second_g(h):
-        give_g(h).wait_recv()
-        start_far(send_far_g, h, other)
-        start_next(send_g, h, other)
-
-    over_heads(second_g, 0, HALF // 2)
-
     for copy in sq_copies:
         copy.wait_recv()
-    over_heads(second_g, HALF // 2)
     give_s.wait_recv()
     send_s.start()
     send_far_s.start()
@@ -291,22 +315,28 @@
 
     over_heads(norm_q)
 
+    def queue_far_q(h):
+        @pl.when(core == 1)
+        def _():
+            give_q(h).wait_recv()
+
+        send_far_q(h).start()
+
     def queue_q(h):
-        start_far(send_far_q, h, core)
         start_next(send_q, h, core)
-        give_q(h).wait_recv()
-        start_far(send_far_q, h, other)
+
+        @pl.when(core == 0)
+        def _():
+            give_q(h).wait_recv()
+
         start_next(send_q, h, other)
 
+    over_heads(queue_far_q)
     over_heads(queue_q)
 
     def pass_g(h):
         send_far_g(h).wait_recv()
         pass_on(g_far, g_next, ng_sem, h)
-
-    @pl.when(core == 0)
-    def _():
-        over_heads(pass_g)
 
     def norm_k(h):
         k_stage[h] = normed(k_all, k_scale, k_gain, other * HALF + h)
@@ -328,43 +358,44 @@
     def group_of(step):
         return (chip * 2 + step) % seq_count
 
-    def key_pos(c):
-        group = group_of(c)
-        row = lax.broadcasted_iota(jnp.int32, (ROWS, ROWS), 0)
-        return row + jnp.where(row < BLK, order[2 * group] * BLK, order[2 * group + 1] * BLK - BLK)
-
-    def query_pos(step):
+    def blocks_of(step):
         group = group_of(step)
-        col = lax.broadcasted_iota(jnp.int32, (1, ROWS), 1)
-        return col + jnp.where(col < BLK, order[2 * group] * BLK, order[2 * group + 1] * BLK - BLK)
-
-    def pair(h, c, q, g, norm_row, delta, q_at):
+        return order[2 * group], order[2 * group + 1]
+
+    def pair(h, c, step, q, g, norm_row, delta):
         s = dot(k_own[h, c], q, NT)
         d = dot(v_own[h, c], g, NT)
-        p = jnp.exp2(s * (score_scale * LOG2E) - norm_row)
-        p = jnp.where(key_pos(c) <= q_at, p, 0.0)
+        query_at, key_at = blocks_of(step), blocks_of(c)
+        col = lax.broadcasted_iota(jnp.int32, (1, ROWS), 1)
+        parts = []
+        for half in range(2):
+            scaled = s[half * BLK : (half + 1) * BLK] * (score_scale * LOG2E)
+            if step == c:
+                query_pos = jnp.where(
+                    col < BLK, query_at[0] * BLK, query_at[1] * BLK - BLK
+                ) + col
+                key_pos = key_at[half] * BLK + lax.broadcasted_iota(jnp.int32, (BLK, ROWS), 0)
+                part = jnp.where(key_pos <= query_pos, jnp.exp2(scaled - norm_row), 0.0)
+            else:
+                hidden = [jnp.where(key_at[half] > at, 1e30, 0.0) for at in query_at]
+                part = jnp.exp2(scaled - (norm_row + jnp.where(col < BLK, hidden[0], hidden[1])))
+            parts.append(part)
+        p = jnp.concatenate(parts, axis=0)
         ds = (p * (d - delta)).astype(BF16)
         dv_add = dot(p.astype(BF16), g, NN)
         dk_add = dot(ds, q, NN)
         dq_add = dot(k_flip[h, c], ds, NN)
         return dq_add, dk_add, dv_add
 
-    def out_copy(stage, out, sem, n, h):
-        mine = pltpu.make_async_copy(
-            stage.at[h, core], out.at[:, head_cols(core * HALF + h)], od_sem.at[n, h]
-        )
-        theirs = remote(
-            stage.at[h, other], out.at[:, head_cols(core * HALF + h)], sem, (h,), sibling
-        )
-        return mine, theirs
-
-    def out_start(stage, out, sem, n, h):
-        for copy in out_copy(stage, out, sem, n, h):
-            copy.start()
-
-    def out_wait(stage, out, sem, n, h):
-        for copy in out_copy(stage, out, sem, n, h):
-            copy.wait()
+    def out_copy(stage, out, sem, h):
+        return remote(
+            stage.at[h], out.at[:, head_cols(core * HALF + h)], sem, (h,), sibling
+        )
+
+    def put(value_of, stage, out, sem, h):
+        stage[h] = value_of(other)
+        out_copy(stage, out, sem, h).start()
+        out[:, head_cols(core * HALF + h)] = value_of(core)
 
     norm_of = lambda ref, g, h: ref[g, pl.ds(h, 1), :]
     delta_of = lambda ref, g, h: ref[g, pl.ds(HALF + h, 1), :]
@@ -373,22 +404,21 @@
         q0, g0, q1, g1 = q_own[h, 0], g_own[h, 0], q_own[h, 1], g_own[h, 1]
         n0, d0 = norm_of(stats, 0, h), delta_of(stats, 0, h)
         n1, d1 = norm_of(stats, 1, h), delta_of(stats, 1, h)
-        dq_add, dk_add, dv_add = pair(h, 0, q0, g0, n0, d0, query_pos(0))
+        dq_add, dk_add, dv_add = pair(h, 0, 0, q0, g0, n0, d0)
         dq_acc[h, 0] = dq_add
         dk_acc[h, 0] = dk_add
         dv_acc[h, 0] = dv_add
-        dq_add, dk_add, dv_add = pair(h, 0, q1, g1, n1, d1, query_pos(1))
+        dq_add, dk_add, dv_add = pair(h, 0, 1, q1, g1, n1, d1)
         dq_acc[h, 1] = dq_add
         dk_acc[h, 0] += dk_add
         dv_acc[h, 0] += dv_add
-        dq_add, dk_add, dv_add = pair(h, 1, q1, g1, n1, d1, query_pos(1))
+        dq_add, dk_add, dv_add = pair(h, 1, 1, q1, g1, n1, d1)
         dq_acc[h, 1] += dq_add
         dk_acc[h, 1] = dk_add
         dv_acc[h, 1] = dv_add
-
-        @pl.when(core == 1)
-        def _():
-            pass_g(h)
+        give_dq(h).start()
+
+        pass_g(h)
 
     over_heads(own)
 
@@ -401,11 +431,11 @@
         dq_add, dk_add, dv_add = pair(
             h,
             1,
+            4,
             q_far[h],
             g_far[h],
             stats_far[pl.ds(h, 1), :],
             stats_far[pl.ds(HALF + h, 1), :],
-            query_pos(4),
         )
         far_stage[h] = dq_add.astype(BF16)
         back_far(h).start()
@@ -417,32 +447,45 @@
             send_q(h, g).wait_recv()
             qn, gn = q_next[h, g], g_next[h, g]
             nn, dn = norm_of(stats_next, g, h), delta_of(stats_next, g, h)
-            first, dk_add, dv_add = pair(h, 0, qn, gn, nn, dn, query_pos(2 + g))
+            first, dk_add, dv_add = pair(h, 0, 2 + g, qn, gn, nn, dn)
             dk_acc[h, 0] += dk_add
             dv_acc[h, 0] += dv_add
-            second, dk_add, dv_add = pair(h, 1, qn, gn, nn, dn, query_pos(2 + g))
+            second, dk_add, dv_add = pair(h, 1, 2 + g, qn, gn, nn, dn)
             dk_acc[h, 1] += dk_add
             dv_acc[h, 1] += dv_add
             next_stage[h, g] = (first + second).astype(BF16)
-            back_next(h, g).start()
-
-        for c in range(2):
-            dk_stage[h, c] = (dk_acc[h, c] * score_scale).astype(BF16)
-            dv_stage[h, c] = dv_acc[h, c].astype(BF16)
-        out_start(dk_stage, dk_out, ok_sem, 0, h)
-        out_start(dv_stage, dv_out, ov_sem, 1, h)
+
+            @pl.when(chip % 2 == 1)
+            def _():
+                back_next(h, g).start()
+
+            @pl.when((chip % 2 == 0) & (h > 0))
+            def _():
+                back_next(h - 1, g).start()
+
+            @pl.when((chip % 2 == 0) & (h == HALF - 1))
+            def _():
+                back_next(h, g).start()
+
+        put(
+            lambda c: (dk_acc[h, c] * score_scale).astype(BF16), dk_stage, dk_out, ok_sem, h
+        )
+        put(lambda c: dv_acc[h, c].astype(BF16), dv_stage, dv_out, ov_sem, h)
 
     over_heads(step)
 
     def finish(h):
-        back_far(h).wait_recv()
-        for g in (1, 0):
-            back_next(h, g).wait_recv()
-            total = dq_acc[h, g] + next_back[h, g].astype(F32)
-            if g == 0:
-                total = total + far_back[h].astype(F32)
-            dq_stage[h, g] = (total * score_scale).T.astype(BF16)
-        out_start(dq_stage, dq_out, oq_sem, 2, h)
+        give_dq(h).wait_recv()
+        for half, total in ((core, dq_acc.at[h, core]), (other, dq_given.at[h])):
+
+            @pl.when(core == 0)
+            def _():
+                back_far_from(h, half).wait_recv()
+                total[...] += far_back[h, half].astype(F32)
+
+            back_next_from(h, half).wait_recv()
+            grad = total[...] + next_back[h, half].astype(F32)
+            dq_out[:, head_cols(half * HALF + h)] = (grad * score_scale).T.astype(BF16)
 
     over_heads(finish)
 
@@ -464,45 +507,37 @@
         send_far_g(h).wait_send()
         send_far_q(h).wait_send()
         back_far(h).wait_send()
-        out_wait(dk_stage, dk_out, ok_sem, 0, h)
-        out_wait(dv_stage, dv_out, ov_sem, 1, h)
-        out_wait(dq_stage, dq_out, oq_sem, 2, h)
+        out_copy(dk_stage, dk_out, ok_sem, h).wait()
+        out_copy(dv_stage, dv_out, ov_sem, h).wait()
+        give_dq(h).wait_send()
 
     over_heads(drain)
 
 
 def store_kernel(*refs):
-    ins, outs, (held, sem_in, sem_out) = refs[:3], refs[3:6], refs[6:]
+    ins, outs, sem = refs[:3], refs[3:6], refs[6]
     half = ROWS // 2
-    parts = [(n, part) for n in range(3) for part in range(2)]
-
-    def load(n, part):
-        rows = pl.ds(part * half, half)
-        return pltpu.make_async_copy(ins[n].at[rows], held.at[n, rows], sem_in.at[n, part])
-
-    def save(n, part):
-        rows = pl.ds(part * half, half)
-        return pltpu.make_async_copy(held.at[n, rows], outs[n].at[rows], sem_out.at[n, part])
-
-    for n, part in parts:
-        load(n, part).start()
-    for n, part in parts:
-        load(n, part).wait()
-        save(n, part).start()
-    for n, part in parts:
-        save(n, part).wait()
+    copies = []
+    for n in range(3):
+        for part in range(2):
+            rows = pl.ds(part * half, half)
+            copies.append(
+                pltpu.make_async_copy(ins[n].at[rows], outs[n].at[rows], sem.at[n, part])
+            )
+    for copy in copies:
+        copy.start()
+    for copy in copies:
+        copy.wait()
 
 
 def store(grads, shape):
-    any_spec = pl.BlockSpec(memory_space=pl.ANY)
-    sem = pltpu.SemaphoreType.DMA
     return pl.pallas_call(
         store_kernel,
         out_shape=(shape,) * 3,
-        in_specs=[any_spec] * 3,
-        out_specs=(any_spec,) * 3,
-        scratch_shapes=[pltpu.VMEM((3, *shape.shape), BF16), sem((3, 2)), sem((3, 2))],
-        compiler_params=pltpu.CompilerParams(vmem_limit_bytes=62 * 1024 * 1024),
+        in_specs=[pl.BlockSpec(memory_space=pltpu.VMEM)] * 3,
+        out_specs=(pl.BlockSpec(memory_space=pl.ANY),) * 3,
+        scratch_shapes=[pltpu.SemaphoreType.DMA((3, 2))],
+        compiler_params=pltpu.CompilerParams(vmem_limit_bytes=4 * 1024 * 1024),
     )(*grads)
 
 
@@ -527,20 +562,20 @@
     scratch += [halves, halves, table, single, single, table_one]
     scratch += [pltpu.VMEM((HALF, 2, HD, ROWS), F32), acc, acc]
     scratch += [flipped, flipped]
-    scratch += [pltpu.VMEM((HALF, HD, ROWS), BF16), pltpu.VMEM((HALF, HD, ROWS), BF16)]
-    scratch += [halves, halves, halves]
+    scratch += [pltpu.VMEM((HALF, HD, ROWS), BF16), flipped]
+    scratch += [pltpu.VMEM((HALF, HD, ROWS), F32), single, single]
     scratch += [sem((4,)), sem((HALF,)), sem((HALF,)), sem((2, head_count))]
     scratch += [sem((2, HALF))] * 4 + [sem((2, 1))]
     scratch += [sem((2, HALF, 2))] * 2 + [sem((2, 1))]
     scratch += [sem((2, HALF))] * 2 + [sem((2, 1))]
-    scratch += [sem((2, HALF, 2)), sem((2, HALF))]
-    scratch += [sem((3, HALF))] + [sem((2, HALF))] * 3
+    scratch += [sem((2, HALF, 2)), sem((2, HALF, 2))]
+    scratch += [sem((2, HALF))] * 3
     shape = jax.ShapeDtypeStruct((rows, columns), BF16)
     grads = pl.pallas_call(
         functools.partial(kernel, seq_count, head_count),
-        out_shape=(shape, shape, shape),
+        out_shape=(whole,) * 3,
         in_specs=[pl.BlockSpec(memory_space=pltpu.SMEM)] + [any_spec] * 5 + [vmem_spec] * 3,
-        out_specs=(any_spec, any_spec, any_spec),
+        out_specs=(vmem_spec,) * 3,
         scratch_shapes=scratch,
         compiler_params=pltpu.CompilerParams(
             collective_id=0, has_side_effects=True, vmem_limit_bytes=62 * 1024 * 1024

time: 59.9 us -> 56.2 us (0.938)
  Pallas kernels: 59.1 us -> 55.4 us
    pallas_call x1, Pallas kernels: 56.9 us -> 54.2 us  [local(): pl.pallas_call(functools.partial(kernel, seq_count, head_count), out_shap...]
    pallas_call x1, Pallas kernels: 2.19 us -> 1.19 us  [store(): pl.pallas_call(store_kernel, out_shape=(shape,) * 3, in_specs=[pl.BlockSp...]
where the time goes in v3:
time: 56.2 us; the launch traced here: 56 us
  Pallas kernels  55.4 us (99%)
  between operations  0.64 us (1%)
    pallas_call x1, Pallas kernels, local(): pl.pallas_call(functools.partial(kernel, seq_count, head_count), out_shap...  54.2 us
    pallas_call x1, Pallas kernels, store(): pl.pallas_call(store_kernel, out_shape=(shape,) * 3, in_specs=[pl.BlockSp...  1.19 us

profile of v3, /device:TPU:1, one launch (start us, length us, event | category | flops | bytes accessed | tf_op | source)
XLA Modules:
  0.0 56.0 jit_solution(5904769468221206927)
XLA Ops:
  0.6 54.2 %shard_map.112 = (bf16[256,1024]{1,0:T(8,128)(2,1)S(1)}, bf16[256,1024]{1,0:T(8,128)(2,1)S(1)}, bf16[256,1024]{1,0:T(8,128)(2,1)S(1)}) custom-call(s32[64]{0:T(128)} %order.1, bf16[256,1024]{1,0:T(8,128)(2,1)} %q_hbm.1, bf16[256,1024]{1,0:T(8,128)(2,1)} %k_hbm.1, bf16[256,1024]{1,0:T(8,128)(2,1)} %v_hbm.1, bf16[256,1024]{1,0:T(8,128)(2,1)} %g_hbm.1, ...), custom_call_target="tpu_custom_call" | custom-call | flops 2684354560 | bytes 4194304 | tf_op jit(solution)/shard_map/pallas_call | solution.py:574
  54.8 1.2 %shard_map.113 = (bf16[256,1024]{1,0:T(8,128)(2,1)}, bf16[256,1024]{1,0:T(8,128)(2,1)}, bf16[256,1024]{1,0:T(8,128)(2,1)}) custom-call(bf16[256,1024]{1,0:T(8,128)(2,1)S(1)} %get-tuple-element.6.refs_0_, bf16[256,1024]{1,0:T(8,128)(2,1)S(1)} %get-tuple-element.7.refs_1_, bf16[256,1024]{1,0:T(8,128)(2,1)S(1)} %get-tuple-element.8.refs_2_), custom_call_target="tpu_custom_call" | custom-call | tf_op jit(solution)/shard_map/pallas_call | solution.py:534

commit v4 on v3

--- a/solution.py
+++ b/solution.py
@@ -20,14 +20,11 @@
 NT = (((1,), (1,)), ((), ()))
 NN = (((1,), (0,)), ((), ()))
 
-
 def dot(a, b, dims):
     return lax.dot_general(a, b, dims, preferred_element_type=F32)
 
-
 def head_cols(head):
     return pl.ds(pl.multiple_of(head * HD, HD), HD)
-
 
 def kernel(
     seq_count,
@@ -156,15 +153,98 @@
             v_hbm.at[:, head_cols(core * HALF + h)], v_own.at[h, core], load_v_sem.at[h]
         )
 
+    for h in range(HALF):
+        load_g(h).start()
     loads[0].start()
     loads[1].start()
-    for h in range(HALF):
-        load_g(h).start()
     loads[2].start()
     loads[3].start()
     for h in range(HALF):
         load_v(h).start()
 
+    pl.semaphore_wait(barrier, 6 + head_count - 1)
+
+    def give_g(h):
+        return remote(
+            g_hbm.at[:, head_cols(other * HALF + h)], g_own.at[h, core], xg_sem, (h,), sibling
+        )
+
+    def give_v(h):
+        return remote(
+            v_hbm.at[:, head_cols(other * HALF + h)], v_own.at[h, core], xv_sem, (h,), sibling
+        )
+
+    def give_q(h):
+        return remote(q_stage.at[h], q_own.at[h, core], xq_sem, (h,), sibling)
+
+    def give_k(h):
+        return remote(k_stage.at[h], k_own.at[h, core], xk_sem, (h,), sibling)
+
+    give_s = remote(stats_stage, stats.at[core], xs_sem, (0,), sibling)
+
+    def send_g(h, g):
+        return remote(g_own.at[h, g], g_next.at[h, g], ng_sem, (h, g), prev)
+
+    def send_q(h, g):
+        return remote(q_own.at[h, g], q_next.at[h, g], nq_sem, (h, g), prev)
+
+    send_s = remote(stats, stats_next, ns_sem, (0,), prev)
+
+    def send_far_g(h):
+        return remote(g_own.at[h, 0], g_far.at[h], fg_sem, (h,), prev_far)
+
+    def send_far_q(h):
+        return remote(q_own.at[h, 0], q_far.at[h], fq_sem, (h,), prev_far)
+
+    send_far_s = remote(stats.at[0], stats_far, fs_sem, (0,), prev_far)
+
+    def back_next(h, g):
+        return remote(
+            next_stage.at[h, g], next_back.at[h, core], nb_sem, (h, g), on_core(succ, g), (h, core)
+        )
+
+    def back_far(h):
+        return remote(
+            far_stage.at[h], far_back.at[h, core], fb_sem, (h, 0), on_core(succ_far, 0), (h, core)
+        )
+
+    def back_next_from(h, half):
+        return remote(
+            next_stage.at[h, 0], next_back.at[h, half], nb_sem, (h, 0), sibling, (h, half)
+        )
+
+    def back_far_from(h, half):
+        return remote(far_stage.at[h], far_back.at[h, half], fb_sem, (h, 0), sibling, (h, half))
+
+    def give_dq(h):
+        return remote(dq_acc.at[h, other], dq_given.at[h], oq_sem, (h,), sibling)
+
+    def over_heads(body, first=0, last=HALF):
+        lax.fori_loop(first, last, lambda h, c: (body(h), c)[1], 0)
+
+    def start_next(send, h, g):
+        @pl.when(g + chip % 2 > 0)
+        def _():
+            send(h, g).start()
+
+    def start_far(send, h, g):
+        @pl.when(g == 0)
+        def _():
+            send(h).start()
+
+    def pass_on(src, dst, sem, h):
+        @pl.when(chip % 2 == 0)
+        def _():
+            remote(src.at[h], dst.at[h, 0], sem, (h, 0), succ).start()
+
+    over_heads(lambda h: give_g(h).start())
+
+    def first_g(h):
+        load_g(h).wait()
+        start_next(send_g, h, core)
+
+    over_heads(first_g, 0, 1)
+
     def row_sums(src):
         def add(h, total):
             block = src[:, head_cols(h)].astype(F32)
@@ -177,88 +257,6 @@
     loads[1].wait()
     squares[0, 0:1, :] = row_sums(q_all)
     squares[0, 1:2, :] = row_sums(k_all)
-    pl.semaphore_wait(barrier, 6 + head_count - 1)
-
-    def give_g(h):
-        return remote(
-            g_hbm.at[:, head_cols(other * HALF + h)], g_own.at[h, core], xg_sem, (h,), sibling
-        )
-
-    def give_v(h):
-        return remote(
-            v_hbm.at[:, head_cols(other * HALF + h)], v_own.at[h, core], xv_sem, (h,), sibling
-        )
-
-    def give_q(h):
-        return remote(q_stage.at[h], q_own.at[h, core], xq_sem, (h,), sibling)
-
-    def give_k(h):
-        return remote(k_stage.at[h], k_own.at[h, core], xk_sem, (h,), sibling)
-
-    give_s = remote(stats_stage, stats.at[core], xs_sem, (0,), sibling)
-
-    def send_g(h, g):
-        return remote(g_own.at[h, g], g_next.at[h, g], ng_sem, (h, g), prev)
-
-    def send_q(h, g):
-        return remote(q_own.at[h, g], q_next.at[h, g], nq_sem, (h, g), prev)
-
-    send_s = remote(stats, stats_next, ns_sem, (0,), prev)
-
-    def send_far_g(h):
-        return remote(g_own.at[h, 0], g_far.at[h], fg_sem, (h,), prev_far)
-
-    def send_far_q(h):
-        return remote(q_own.at[h, 0], q_far.at[h], fq_sem, (h,), prev_far)
-
-    send_far_s = remote(stats.at[0], stats_far, fs_sem, (0,), prev_far)
-
-    def back_next(h, g):
-        return remote(
-            next_stage.at[h, g], next_back.at[h, core], nb_sem, (h, g), on_core(succ, g), (h, core)
-        )
-
-    def back_far(h):
-        return remote(
-            far_stage.at[h], far_back.at[h, core], fb_sem, (h, 0), on_core(succ_far, 0), (h, core)
-        )
-
-    def back_next_from(h, half):
-        return remote(
-            next_stage.at[h, 0], next_back.at[h, half], nb_sem, (h, 0), sibling, (h, half)
-        )
-
-    def back_far_from(h, half):
-        return remote(far_stage.at[h], far_back.at[h, half], fb_sem, (h, 0), sibling, (h, half))
-
-    def give_dq(h):
-        return remote(dq_acc.at[h, other], dq_given.at[h], oq_sem, (h,), sibling)
-
-    def over_heads(body, first=0, last=HALF):
-        lax.fori_loop(first, last, lambda h, c: (body(h), c)[1], 0)
-
-    def start_next(send, h, g):
-        @pl.when(g + chip % 2 > 0)
-        def _():
-            send(h, g).start()
-
-    def start_far(send, h, g):
-        @pl.when(g == 0)
-        def _():
-            send(h).start()
-
-    def pass_on(src, dst, sem, h):
-        @pl.when(chip % 2 == 0)
-        def _():
-            remote(src.at[h], dst.at[h, 0], sem, (h, 0), succ).start()
-
-    over_heads(lambda h: give_g(h).start())
-
-    def first_g(h):
-        load_g(h).wait()
-        start_next(send_g, h, core)
-
-
     sq_copies = []
     for n in range(1, head_count):
         copy = remote(
@@ -267,7 +265,7 @@
         copy.start()
         sq_copies.append(copy)
 
-    over_heads(first_g)
+    over_heads(first_g, 1)
     over_heads(lambda h: give_v(h).start())
 
     def second_g(h):
@@ -370,7 +368,7 @@
         parts = []
         for half in range(2):
             scaled = s[half * BLK : (half + 1) * BLK] * (score_scale * LOG2E)
-            if step == c:
+            if isinstance(step, int) and step == c:
                 query_pos = jnp.where(
                     col < BLK, query_at[0] * BLK, query_at[1] * BLK - BLK
                 ) + col
@@ -425,7 +423,7 @@
     send_far_s.wait_recv()
     send_s.wait_recv()
 
-    def step(h):
+    def far_step(h):
         send_far_q(h).wait_recv()
         pass_on(q_far, q_next, nq_sem, h)
         dq_add, dk_add, dv_add = pair(
@@ -442,7 +440,13 @@
         dk_acc[h, 1] += dk_add
         dv_acc[h, 1] += dv_add
 
-        for g in (1, 0):
+    over_heads(far_step)
+
+    first_in = jnp.where(chip % 2 == 1, 0, core)
+
+    def step(h):
+        def next_group(n, carry):
+            g = lax.rem(first_in + n, 2)
             send_g(h, g).wait_recv()
             send_q(h, g).wait_recv()
             qn, gn = q_next[h, g], g_next[h, g]
@@ -455,17 +459,10 @@
             dv_acc[h, 1] += dv_add
             next_stage[h, g] = (first + second).astype(BF16)
 
-            @pl.when(chip % 2 == 1)
-            def _():
-                back_next(h, g).start()
-
-            @pl.when((chip % 2 == 0) & (h > 0))
-            def _():
-                back_next(h - 1, g).start()
-
-            @pl.when((chip % 2 == 0) & (h == HALF - 1))
-            def _():
-                back_next(h, g).start()
+            back_next(h, g).start()
+            return carry
+
+        lax.fori_loop(0, 2, next_group, 0)
 
         put(
             lambda c: (dk_acc[h, c] * score_scale).astype(BF16), dk_stage, dk_out, ok_sem, h
@@ -513,7 +510,6 @@
 
     over_heads(drain)
 
-
 def store_kernel(*refs):
     ins, outs, sem = refs[:3], refs[3:6], refs[6]
     half = ROWS // 2
@@ -529,7 +525,6 @@
     for copy in copies:
         copy.wait()
 
-
 def store(grads, shape):
     return pl.pallas_call(
         store_kernel,
@@ -539,7 +534,6 @@
         scratch_shapes=[pltpu.SemaphoreType.DMA((3, 2))],
         compiler_params=pltpu.CompilerParams(vmem_limit_bytes=4 * 1024 * 1024),
     )(*grads)
-
 
 def local(q_raw, k_raw, values, out_grad, attn_out, log_norm, q_gain, k_gain, order):
     seq_count = lax.axis_size("seq")
@@ -598,7 +592,6 @@
     )
     return store(grads, shape)
 
-
 def solution(mesh):
     placed = P("seq", "head")
     return jax.shard_map(

time: 56.2 us -> 52.8 us (0.940)
  Pallas kernels: 55.4 us -> 52 us
    pallas_call x1, Pallas kernels: 54.2 us -> 50.8 us  [local(): pl.pallas_call(functools.partial(kernel, seq_count, head_count), out_shap...]
where the time goes in v4:
time: 52.8 us; the launch traced here: 52.7 us
  Pallas kernels  52 us (98%)
  between operations  0.64 us (1%)
    pallas_call x1, Pallas kernels, local(): pl.pallas_call(functools.partial(kernel, seq_count, head_count), out_shap...  50.8 us
    pallas_call x1, Pallas kernels, store(): pl.pallas_call(store_kernel, out_shape=(shape,) * 3, in_specs=[pl.BlockSp...  1.19 us

profile of v4, /device:TPU:1, one launch (start us, length us, event | category | flops | bytes accessed | tf_op | source)
XLA Modules:
  0.0 52.7 jit_solution(10986935551661918540)
XLA Ops:
  0.6 50.8 %shard_map.112 = (bf16[256,1024]{1,0:T(8,128)(2,1)S(1)}, bf16[256,1024]{1,0:T(8,128)(2,1)S(1)}, bf16[256,1024]{1,0:T(8,128)(2,1)S(1)}) custom-call(s32[64]{0:T(128)} %order.1, bf16[256,1024]{1,0:T(8,128)(2,1)} %q_hbm.1, bf16[256,1024]{1,0:T(8,128)(2,1)} %k_hbm.1, bf16[256,1024]{1,0:T(8,128)(2,1)} %v_hbm.1, bf16[256,1024]{1,0:T(8,128)(2,1)} %g_hbm.1, ...), custom_call_target="tpu_custom_call" | custom-call | flops 2684354560 | bytes 4194304 | tf_op jit(solution)/shard_map/pallas_call | solution.py:568
  51.5 1.2 %shard_map.113 = (bf16[256,1024]{1,0:T(8,128)(2,1)}, bf16[256,1024]{1,0:T(8,128)(2,1)}, bf16[256,1024]{1,0:T(8,128)(2,1)}) custom-call(bf16[256,1024]{1,0:T(8,128)(2,1)S(1)} %get-tuple-element.6.refs_0_, bf16[256,1024]{1,0:T(8,128)(2,1)S(1)} %get-tuple-element.7.refs_1_, bf16[256,1024]{1,0:T(8,128)(2,1)S(1)} %get-tuple-element.8.refs_2_), custom_call_target="tpu_custom_call" | custom-call | tf_op jit(solution)/shard_map/pallas_call | solution.py:529

commit v5 on v4

--- a/solution.py
+++ b/solution.py
@@ -162,6 +162,39 @@
     for h in range(HALF):
         load_v(h).start()
 
+    def row_sums(src):
+        def add(h, total):
+            block = src[:, head_cols(h)].astype(F32)
+            return total + block * block
+
+        total = lax.fori_loop(0, 2 * HALF, add, jnp.zeros((ROWS, HD), F32))
+        return jnp.sum(total.T, axis=0, keepdims=True)
+
+    def sum_squares():
+        loads[0].wait()
+        loads[1].wait()
+        squares[0, 0:1, :] = row_sums(q_all)
+        squares[0, 1:2, :] = row_sums(k_all)
+
+    def make_stats():
+        loads[2].wait()
+        loads[3].wait()
+        norm_rows = norm_ref[...] * LOG2E
+
+        def delta_row(h):
+            product = g_all[:, head_cols(h)].astype(F32) * o_all[:, head_cols(h)].astype(F32)
+            return jnp.sum(product.T, axis=0, keepdims=True)
+
+        first_half = core == 0
+        stats[core, 0:HALF, :] = jnp.where(first_half, norm_rows[0:HALF], norm_rows[HALF:])
+        stats_stage[0:HALF, :] = jnp.where(first_half, norm_rows[HALF:], norm_rows[0:HALF])
+        for h in range(HALF):
+            stats[core, HALF + h : HALF + h + 1, :] = delta_row(core * HALF + h)
+            stats_stage[HALF + h : HALF + h + 1, :] = delta_row(other * HALF + h)
+
+    sum_squares()
+    make_stats()
+
     pl.semaphore_wait(barrier, 6 + head_count - 1)
 
     def give_g(h):
@@ -237,26 +270,10 @@
         def _():
             remote(src.at[h], dst.at[h, 0], sem, (h, 0), succ).start()
 
-    over_heads(lambda h: give_g(h).start())
-
     def first_g(h):
         load_g(h).wait()
         start_next(send_g, h, core)
 
-    over_heads(first_g, 0, 1)
-
-    def row_sums(src):
-        def add(h, total):
-            block = src[:, head_cols(h)].astype(F32)
-            return total + block * block
-
-        total = lax.fori_loop(0, 2 * HALF, add, jnp.zeros((ROWS, HD), F32))
-        return jnp.sum(total.T, axis=0, keepdims=True)
-
-    loads[0].wait()
-    loads[1].wait()
-    squares[0, 0:1, :] = row_sums(q_all)
-    squares[0, 1:2, :] = row_sums(k_all)
     sq_copies = []
     for n in range(1, head_count):
         copy = remote(
@@ -265,7 +282,9 @@
         copy.start()
         sq_copies.append(copy)
 
-    over_heads(first_g, 1)
+    give_s.start()
+    over_heads(lambda h: give_g(h).start())
+    over_heads(first_g)
     over_heads(lambda h: give_v(h).start())
 
     def second_g(h):
@@ -274,22 +293,6 @@
 
     over_heads(second_g)
     over_heads(lambda h: send_far_g(h).start())
-
-    loads[2].wait()
-    loads[3].wait()
-    norm_rows = norm_ref[...] * LOG2E
-
-    def delta_row(h):
-        product = g_all[:, head_cols(h)].astype(F32) * o_all[:, head_cols(h)].astype(F32)
-        return jnp.sum(product.T, axis=0, keepdims=True)
-
-    first_half = core == 0
-    stats[core, 0:HALF, :] = jnp.where(first_half, norm_rows[0:HALF], norm_rows[HALF:])
-    stats_stage[0:HALF, :] = jnp.where(first_half, norm_rows[HALF:], norm_rows[0:HALF])
-    for h in range(HALF):
-        stats[core, HALF + h : HALF + h + 1, :] = delta_row(core * HALF + h)
-        stats_stage[HALF + h : HALF + h + 1, :] = delta_row(other * HALF + h)
-    give_s.start()
 
     for copy in sq_copies:
         copy.wait_recv()
@@ -442,7 +445,7 @@
 
     over_heads(far_step)
 
-    first_in = jnp.where(chip % 2 == 1, 0, core)
+    first_in = jnp.where(chip % 2 == 1, 1, core)
 
     def step(h):
         def next_group(n, carry):

time: 52.8 us -> 51.5 us (0.975); the launches traced: 52.7 us -> 50.5 us
  Pallas kernels: 52 us -> 49.9 us
    pallas_call x1, Pallas kernels: 50.8 us -> 48.7 us  [local(): pl.pallas_call(functools.partial(kernel, seq_count, head_count), out_shap...]
where the time goes in v5:
time: 51.5 us; the launch traced here: 50.5 us
  Pallas kernels  49.9 us (97%)
  between operations  0.64 us (1%)
    pallas_call x1, Pallas kernels, local(): pl.pallas_call(functools.partial(kernel, seq_count, head_count), out_shap...  48.7 us
    pallas_call x1, Pallas kernels, store(): pl.pallas_call(store_kernel, out_shape=(shape,) * 3, in_specs=[pl.BlockSp...  1.19 us

profile of v5, /device:TPU:1, one launch (start us, length us, event | category | flops | bytes accessed | tf_op | source)
XLA Modules:
  0.0 50.5 jit_solution(2135853370274445304)
XLA Ops:
  0.6 48.7 %shard_map.112 = (bf16[256,1024]{1,0:T(8,128)(2,1)S(1)}, bf16[256,1024]{1,0:T(8,128)(2,1)S(1)}, bf16[256,1024]{1,0:T(8,128)(2,1)S(1)}) custom-call(s32[64]{0:T(128)} %order.1, bf16[256,1024]{1,0:T(8,128)(2,1)} %q_hbm.1, bf16[256,1024]{1,0:T(8,128)(2,1)} %k_hbm.1, bf16[256,1024]{1,0:T(8,128)(2,1)} %v_hbm.1, bf16[256,1024]{1,0:T(8,128)(2,1)} %g_hbm.1, ...), custom_call_target="tpu_custom_call" | custom-call | flops 2684354560 | bytes 4194304 | tf_op jit(solution)/shard_map/pallas_call | solution.py:571
  49.3 1.2 %shard_map.113 = (bf16[256,1024]{1,0:T(8,128)(2,1)}, bf16[256,1024]{1,0:T(8,128)(2,1)}, bf16[256,1024]{1,0:T(8,128)(2,1)}) custom-call(bf16[256,1024]{1,0:T(8,128)(2,1)S(1)} %get-tuple-element.6.refs_0_, bf16[256,1024]{1,0:T(8,128)(2,1)S(1)} %get-tuple-element.7.refs_1_, bf16[256,1024]{1,0:T(8,128)(2,1)S(1)} %get-tuple-element.8.refs_2_), custom_call_target="tpu_custom_call" | custom-call | tf_op jit(solution)/shard_map/pallas_call | solution.py:532

commit v6 on v5

--- a/solution.py
+++ b/solution.py
@@ -332,8 +332,20 @@
 
         start_next(send_q, h, other)
 
-    over_heads(queue_far_q)
-    over_heads(queue_q)
+    def queue_odd_q(h):
+        send_q(h, core).start()
+        give_q(h).wait_recv()
+        send_q(h, other).start()
+        send_far_q(h).start()
+
+    @pl.when(chip % 2 == 0)
+    def _():
+        over_heads(queue_far_q)
+        over_heads(queue_q)
+
+    @pl.when(chip % 2 == 1)
+    def _():
+        over_heads(queue_odd_q)
 
     def pass_g(h):
         send_far_g(h).wait_recv()

time: 51.5 us -> 51.5 us (level)
  no operation moved by 1% of the time
where the time goes in v6:
time: 51.5 us; the launch traced here: 50.5 us
  Pallas kernels  49.9 us (97%)
  between operations  0.64 us (1%)
    pallas_call x1, Pallas kernels, local(): pl.pallas_call(functools.partial(kernel, seq_count, head_count), out_shap...  48.7 us
    pallas_call x1, Pallas kernels, store(): pl.pallas_call(store_kernel, out_shape=(shape,) * 3, in_specs=[pl.BlockSp...  1.19 us

profile of v6, /device:TPU:1, one launch (start us, length us, event | category | flops | bytes accessed | tf_op | source)
XLA Modules:
  0.0 50.5 jit_solution(4317360810496956694)
XLA Ops:
  0.6 48.7 %shard_map.112 = (bf16[256,1024]{1,0:T(8,128)(2,1)S(1)}, bf16[256,1024]{1,0:T(8,128)(2,1)S(1)}, bf16[256,1024]{1,0:T(8,128)(2,1)S(1)}) custom-call(s32[64]{0:T(128)} %order.1, bf16[256,1024]{1,0:T(8,128)(2,1)} %q_hbm.1, bf16[256,1024]{1,0:T(8,128)(2,1)} %k_hbm.1, bf16[256,1024]{1,0:T(8,128)(2,1)} %v_hbm.1, bf16[256,1024]{1,0:T(8,128)(2,1)} %g_hbm.1, ...), custom_call_target="tpu_custom_call" | custom-call | flops 2684354560 | bytes 4194304 | tf_op jit(solution)/shard_map/pallas_call | solution.py:583
  49.3 1.2 %shard_map.113 = (bf16[256,1024]{1,0:T(8,128)(2,1)}, bf16[256,1024]{1,0:T(8,128)(2,1)}, bf16[256,1024]{1,0:T(8,128)(2,1)}) custom-call(bf16[256,1024]{1,0:T(8,128)(2,1)S(1)} %get-tuple-element.6.refs_0_, bf16[256,1024]{1,0:T(8,128)(2,1)S(1)} %get-tuple-element.7.refs_1_, bf16[256,1024]{1,0:T(8,128)(2,1)S(1)} %get-tuple-element.8.refs_2_), custom_call_target="tpu_custom_call" | custom-call | tf_op jit(solution)/shard_map/pallas_call | solution.py:544
